TPU v7x, 128 devices: a whole 4x4x4 slice. The times are simulated.
128 devices in a mesh: role: 2 (over core), row: 4 (over x), col: 16 (over z, y).
Axes of the slice: x: 4, y: 4, z: 4, core: 2. Of those that a mesh axis runs over, the one named last changes fastest.
Arguments:
- queries: bfloat16 [128, 32, 4096], P(('role', 'row', 'col')), may hold values from -6 to 6
- cache_keys: bfloat16 [128, 4096, 512], P(('role', 'row', 'col')), may hold values from -6 to 6
- prompt_value_cache: bfloat16 [128, 4096, 512], P(('role', 'row', 'col')), may hold values from -6 to 6
- new_keys: bfloat16 [128, 32, 512], P(('role', 'row', 'col')), may hold values from -6 to 6
- fresh_token_values: bfloat16 [128, 32, 512], P(('role', 'row', 'col')), may hold values from -6 to 6
- hidden: bfloat16 [128, 32, 2048], P(('role', 'row', 'col')), may hold values from -6 to 6
- out_weight: bfloat16 [4096, 2048], P('row'), may hold values from -0.09375 to 0.09375
- norm_gain: float32 [2048], replicated, may hold values from 0.1 to 1.9
- expert_gate: bfloat16 [128, 2048, 768], P(('role', 'row', 'col')), may hold values from -0.125 to 0.125
- expert_up: bfloat16 [128, 2048, 768], P(('role', 'row', 'col')), may hold values from -0.125 to 0.125
- expert_down: bfloat16 [128, 768, 2048], P(('role', 'row', 'col')), may hold values from -0.21875 to 0.21875
- expert_ids: int32 [128, 32, 8], P(('role', 'row', 'col')), may hold values from 0 to 127, all different within a row; in each aligned block of 32 rows (0 to 31, 32 to 63, ..., all dimensions but the last counted through in order) at most 5 rows name the same one
- routing_gates: float32 [128, 32, 8], P(('role', 'row', 'col')), may hold values from 0.1 to 1
Outputs:
- layer_out: bfloat16 [128, 32, 2048], P(('role', 'row', 'col'))
Inputs may be any that keep to these rules, and one draw needn't show every extreme that they name: `expert_ids`: each row names 8 different experts; in the 32 rows of one prompt no expert is named more than 5 times, a bound that some block reaches; every expert is named by some row.
All inputs are finite; a program needn't handle non-finite values.
Results may differ from a plain program's by a relative error of at most 0.014.
Values may be sent and summed in bfloat16 or wider, within the bound.
A program may use at most 128 MiB of HBM per device.

v0:
```python
import jax
import jax.numpy as jnp
from jax import lax
from jax.sharding import PartitionSpec as P

QUERY_HEADS = 32
KEY_VALUE_HEADS = 4
HEAD_SIZE = 128


def attend_prompt(query_rows, keys_cache, values_cache, keys_new, values_new):
    row_count = query_rows.shape[0]
    heads_per_group = QUERY_HEADS // KEY_VALUE_HEADS
    score_scale = HEAD_SIZE ** (-0.5)
    pieces = []
    for key_value_head in range(KEY_VALUE_HEADS):
        first_col = key_value_head * heads_per_group * HEAD_SIZE
        q_block = query_rows[:, first_col : first_col + heads_per_group * HEAD_SIZE].reshape(
            row_count * heads_per_group, HEAD_SIZE
        )
        k_block = keys_cache[:, key_value_head * HEAD_SIZE : (key_value_head + 1) * HEAD_SIZE]
        v_block = values_cache[:, key_value_head * HEAD_SIZE : (key_value_head + 1) * HEAD_SIZE]
        own_key = jnp.repeat(
            keys_new[:, key_value_head * HEAD_SIZE : (key_value_head + 1) * HEAD_SIZE],
            heads_per_group,
            axis=0,
        )
        own_value = jnp.repeat(
            values_new[:, key_value_head * HEAD_SIZE : (key_value_head + 1) * HEAD_SIZE],
            heads_per_group,
            axis=0,
        )
        scores = (
            jnp.einsum("qd,kd->qk", q_block, k_block, preferred_element_type=jnp.float32)
            * score_scale
        )
        own_score = (
            jnp.sum(q_block.astype(jnp.float32) * own_key.astype(jnp.float32), axis=1) * score_scale
        )
        highest = jnp.maximum(jnp.max(scores, axis=1), own_score)
        exp_scores = jnp.exp(scores - highest[:, None])
        own_exp = jnp.exp(own_score - highest)
        denominator = jnp.sum(exp_scores, axis=1) + own_exp
        weights = (exp_scores / denominator[:, None]).astype(jnp.bfloat16)
        own_weight = (own_exp / denominator).astype(jnp.bfloat16)
        mixed_rows = jnp.dot(weights, v_block, preferred_element_type=jnp.float32)
        mixed_rows = mixed_rows + own_weight.astype(jnp.float32)[:, None] * own_value.astype(
            jnp.float32
        )
        pieces.append(
            mixed_rows.astype(jnp.bfloat16).reshape(row_count, heads_per_group * HEAD_SIZE)
        )
    return jnp.concatenate(pieces, axis=1)


def per_device(
    queries,
    cache_keys,
    prompt_value_cache,
    new_keys,
    fresh_token_values,
    hidden,
    out_weight,
    norm_gain,
    expert_gate,
    expert_up,
    expert_down,
    expert_ids,
    routing_gates,
):
    attended = attend_prompt(
        queries[0], cache_keys[0], prompt_value_cache[0], new_keys[0], fresh_token_values[0]
    )
    row_count = attended.shape[0]
    width = hidden.shape[2]
    head_parts = lax.all_to_all(attended, "row", split_axis=1, concat_axis=0, tiled=True)
    projected = lax.psum_scatter(
        jnp.dot(head_parts, out_weight, preferred_element_type=jnp.float32).astype(jnp.bfloat16),
        "row",
        scatter_dimension=0,
        tiled=True,
    ).astype(jnp.float32)
    mid_rows = hidden[0].astype(jnp.float32) + projected
    mean_square = jnp.mean(mid_rows * mid_rows, axis=1, keepdims=True)
    normed = (mid_rows * lax.rsqrt(mean_square + 1e-06) * norm_gain[None, :]).astype(jnp.bfloat16)
    group_rows = lax.axis_size("role") * lax.axis_size("row")
    group_cols = lax.axis_size("col")
    experts = group_rows * group_cols
    top_count = expert_ids.shape[2]
    capacity = row_count * top_count * 3 // (2 * experts) + 2
    flat_ids = expert_ids[0].reshape(row_count * top_count)
    onehot = (flat_ids[:, None] == jnp.arange(experts, dtype=jnp.int32)[None, :]).astype(jnp.int32)
    rank_before = jnp.cumsum(onehot, axis=0) - onehot
    slot_index = jnp.sum(rank_before * onehot, axis=1)
    position = flat_ids * capacity + slot_index
    match_table = (
        position.reshape(row_count, top_count)[None, :, :]
        == jnp.arange(experts * capacity, dtype=jnp.int32)[:, None, None]
    )
    dispatch_matrix = jnp.any(match_table, axis=2).astype(jnp.bfloat16)
    send_rows = jnp.dot(dispatch_matrix, normed, preferred_element_type=jnp.float32).astype(
        jnp.bfloat16
    )
    send_rows = send_rows.reshape(experts, capacity, width)
    gate_matrix = expert_gate[0]
    up_matrix = expert_up[0]
    down_matrix = expert_down[0]
    block = lax.all_to_all(
        send_rows, ("role", "row", "col"), split_axis=0, concat_axis=0, tiled=True
    )
    flat_block = block.reshape(-1, width)
    gate_part = jnp.dot(flat_block, gate_matrix, preferred_element_type=jnp.float32)
    up_part = jnp.dot(flat_block, up_matrix, preferred_element_type=jnp.float32)
    act = (jax.nn.silu(gate_part) * up_part).astype(jnp.bfloat16)
    result_rows = jnp.dot(act, down_matrix, preferred_element_type=jnp.float32).astype(jnp.bfloat16)
    returned = lax.all_to_all(
        result_rows.reshape(block.shape),
        ("role", "row", "col"),
        split_axis=0,
        concat_axis=0,
        tiled=True,
    )
    picked = jnp.take(returned.reshape(experts * capacity, width), position, axis=0)
    picked = picked.reshape(row_count, top_count, width).astype(jnp.float32)
    expert_sum = jnp.sum(picked * routing_gates[0][:, :, None], axis=1)
    return (mid_rows + expert_sum).astype(jnp.bfloat16)[None]


def solution(mesh):
    return jax.shard_map(
        per_device,
        mesh=mesh,
        in_specs=(
            P(("role", "row", "col"), None, None),
            P(("role", "row", "col"), None, None),
            P(("role", "row", "col"), None, None),
            P(("role", "row", "col"), None, None),
            P(("role", "row", "col"), None, None),
            P(("role", "row", "col"), None, None),
            P("row", None),
            P(),
            P(("role", "row", "col"), None, None),
            P(("role", "row", "col"), None, None),
            P(("role", "row", "col"), None, None),
            P(("role", "row", "col"), None, None),
            P(("role", "row", "col"), None, None),
        ),
        out_specs=P(("role", "row", "col"), None, None),
        check_vma=False,
    )
```

profile of v0, /device:TPU:0, one launch (start us, length us, event | category | flops | bytes accessed | tf_op | source)
XLA Modules:
  0.0 261.4 jit_solution(10229751703460542333)
XLA Ops:
  7.4 1.5 slice_convert_fusion.6
  8.9 1.0 fusion.56
  10.0 2.0 fusion.60
  12.0 3.9 %fusion.59 = (f32[256]{0:T(256)S(1)}, f32[256,4096]{1,0:T(8,128)}) fusion(bf16[256,128]{1,0:T(8,128)(2,1)S(1)} %reshape.227, bf16[4096,512]{1,0:T(8,128)(2,1)} %bitcast.101), kind=kOutput, calls=%fused_computation.121 | convolution fusion | flops 270532352 | bytes 5309440 | tf_op jit(solution)/shard_map/qd,kd->qk/dot_general | solution.py:34
  16.8 2.3 fusion.19
  19.2 3.0 %fusion.1 = f32[256]{0:T(256)S(1)} fusion(f32[256,4096]{1,0:T(8,128)} %get-tuple-element.32, f32[256]{0:T(256)S(1)} %multiply_maximum_fusion.2), kind=kLoop, calls=%fused_computation.14 | loop fusion | flops 2096896 | bytes 4196352 | tf_op jit(solution)/shard_map/reduce_sum | solution.py:43
  22.6 2.2 fusion.20
  24.9 2.0 fusion.58
  26.9 3.9 %fusion.57 = (f32[256]{0:T(256)S(1)}, f32[256,4096]{1,0:T(8,128)}) fusion(bf16[256,128]{1,0:T(8,128)(2,1)S(1)} %reshape.229, bf16[4096,512]{1,0:T(8,128)(2,1)} %bitcast.103), kind=kOutput, calls=%fused_computation.119 | convolution fusion | flops 270532352 | bytes 5309440 | tf_op jit(solution)/shard_map/qd,kd->qk/dot_general | solution.py:34
  31.7 2.3 fusion.21
  34.0 3.0 %fusion.3 = f32[256]{0:T(256)S(1)} fusion(f32[256,4096]{1,0:T(8,128)} %get-tuple-element.28, f32[256]{0:T(256)S(1)} %multiply_maximum_fusion), kind=kLoop, calls=%fused_computation.16 | loop fusion | flops 2096896 | bytes 4196352 | tf_op jit(solution)/shard_map/reduce_sum | solution.py:43
  37.4 2.9 %fusion.22 = bf16[256,128]{1,0:T(8,128)(2,1)} fusion(f32[256,4096]{1,0:T(8,128)S(1)} %copy-done.1, f32[256]{0:T(256)S(1)} %get-tuple-element.26, f32[256]{0:T(256)S(1)} %multiply_maximum_fusion, bf16[4096,512]{1,0:T(8,128)(2,1)} %bitcast.117, f32[32,128]{1,0:T(8,128)S(1)} %get-tuple-element.10, f32[256]{0:T(256)S(1)} %get-tuple-element.25), kind=kOutput, calls=%fused_computation.38 | convolution fusion | flops 271679488 | bytes 5327872 | tf_op jit(solution)/shard_map/dot_general | solution.py:46
  40.3 0.9 concatenate.15
  42.0 4.4 %all-to-all-start = ((bf16[32,4,1024]{2,0,1:T(8,128)(2,1)}), bf16[32,4,1024]{2,0,1:T(8,128)(2,1)S(1)}, u32[]{:S(2)}, u32[]{:S(2)}) async-start(bf16[32,4,1024]{2,0,1:T(8,128)(2,1)} %pad_maximum_fusion), calls=%async_computation | async-start | bytes 524288 | tf_op jit(solution)/shard_map/all_to_all | solution.py:76
  48.4 1.4 copy.26
  49.8 3.2 %all-to-all-done = bf16[32,4,1024]{2,0,1:T(8,128)(2,1)S(1)} async-done(((bf16[32,4,1024]{2,0,1:T(8,128)(2,1)}), bf16[32,4,1024]{2,0,1:T(8,128)(2,1)S(1)}, u32[]{:S(2)}, u32[]{:S(2)}) %all-to-all-start) | async-done | bytes 262176 | tf_op jit(solution)/shard_map/all_to_all | solution.py:76
  53.0 3.7 %convolution_convert_fusion.2 = bf16[128,2048]{1,0:T(8,128)(2,1)} fusion(bf16[128,1024]{1,0:T(8,128)(2,1)S(1)} %bitcast.104, bf16[1024,2048]{1,0:T(8,128)(2,1)} %param.19), kind=kOutput, calls=%fused_computation.24 | convolution fusion | flops 537133056 | bytes 4980736 | tf_op jit(solution)/shard_map/dot_general | solution.py:78
  56.7 1.0 fusion.34
  59.1 19.7 %reduce-scatter.2.cloned.1.call-done = bf16[32,2048]{1,0:T(8,128)(2,1)} async-done(((bf16[128,2048]{1,0:T(8,128)(2,1)}), bf16[32,2048]{1,0:T(8,128)(2,1)}) %reduce-scatter.2.cloned.1.call-update) | async-done | bytes 131088 | tf_op jit(solution)/shard_map/reduce_scatter | solution.py:77
  78.8 1.1 multiply_reduce_fusion.1
  79.9 3.4 %convolution_convert_fusion.1 = bf16[640,2048]{1,0:T(8,128)(2,1)} fusion(pred[640,32]{0,1:T(8,128)(4,1)S(1)} %fusion.33, bf16[32,2048]{1,0:T(8,128)(2,1)} %reduce-scatter.2.cloned.1.call-done, bf16[1,32,2048]{2,1,0:T(8,128)(2,1)S(1)} %copy-done.3, f32[2048]{0:T(1024)} %param.20, f32[32]{0:T(128)S(1)} %add_rsqrt_fusion), kind=kOutput, calls=%fused_computation.18 | convolution fusion | flops 85590016 | bytes 2912384 | tf_op jit(solution)/shard_map/dot_general | solution.py:101
  83.2 5.4 %reshape.231 = bf16[128,5,2048]{2,1,0:T(8,128)(2,1)} reshape(bf16[640,2048]{1,0:T(8,128)(2,1)} %convolution_convert_fusion.1) | data formatting | bytes 5242880 | tf_op jit(solution)/shard_map/reshape | solution.py:104
  88.7 62.3 %all_to_all.26 = bf16[128,5,2048]{2,1,0:T(8,128)(2,1)} all-to-all(bf16[128,5,2048]{2,1,0:T(8,128)(2,1)} %reshape.231), channel_id=1, replica_groups=mesh['role'=2,'row'=4,'col'=16] {'role','row','col'}, dimensions={0} | all-to-all | bytes 5242880 | tf_op jit(solution)/shard_map/all_to_all | solution.py:108
  151.0 5.6 %reshape.232 = bf16[640,2048]{1,0:T(8,128)(2,1)} reshape(bf16[128,5,2048]{2,1,0:T(8,128)(2,1)} %all_to_all.26) | data formatting | bytes 5242880 | tf_op jit(solution)/shard_map/reshape | solution.py:111
  156.6 6.2 %fusion.7 = f32[640,768]{1,0:T(8,128)} fusion(bf16[640,2048]{1,0:T(8,128)(2,1)} %reshape.232, bf16[1,2048,768]{2,1,0:T(8,128)(2,1)} %param.21), kind=kOutput, calls=%fused_computation.22 | convolution fusion | flops 2013265920 | bytes 7733248 | tf_op jit(solution)/shard_map/dot_general | solution.py:112
  162.8 9.6 %convolution_convert_fusion = bf16[640,2048]{1,0:T(8,128)(2,1)} fusion(bf16[1,768,2048]{2,1,0:T(8,128)(2,1)S(1)} %copy-done, f32[640,768]{1,0:T(8,128)} %fusion.7, bf16[640,2048]{1,0:T(8,128)(2,1)} %reshape.232, bf16[1,2048,768]{2,1,0:T(8,128)(2,1)} %param.22), kind=kOutput, calls=%fused_computation.17 | convolution fusion | flops 4030791680 | bytes 13500416 | tf_op jit(solution)/shard_map/dot_general | solution.py:115
  172.4 5.5 %reshape.233 = bf16[128,5,2048]{2,1,0:T(8,128)(2,1)} reshape(bf16[640,2048]{1,0:T(8,128)(2,1)} %convolution_convert_fusion) | data formatting | bytes 5242880 | tf_op jit(solution)/shard_map/reshape | solution.py:117
  177.9 9.1 %all-to-all-start.2 = ((bf16[128,5,2048]{2,1,0:T(8,128)(2,1)}), bf16[128,5,2048]{2,1,0:T(8,128)(2,1)}, u32[]{:S(2)}, u32[]{:S(2)}) async-start(bf16[128,5,2048]{2,1,0:T(8,128)(2,1)} %reshape.233), calls=%async_computation.3 | async-start | bytes 8388608 | tf_op jit(solution)/shard_map/all_to_all | solution.py:116
  187.3 52.8 %all-to-all-done.2 = bf16[128,5,2048]{2,1,0:T(8,128)(2,1)} async-done(((bf16[128,5,2048]{2,1,0:T(8,128)(2,1)}), bf16[128,5,2048]{2,1,0:T(8,128)(2,1)}, u32[]{:S(2)}, u32[]{:S(2)}) %all-to-all-start.2) | async-done | bytes 2621472 | tf_op jit(solution)/shard_map/all_to_all | solution.py:116
  240.1 5.6 %reshape.234 = bf16[640,2048]{1,0:T(8,128)(2,1)} reshape(bf16[128,5,2048]{2,1,0:T(8,128)(2,1)} %all-to-all-done.2) | data formatting | bytes 5242880 | tf_op jit(solution)/shard_map/reshape | solution.py:123
  245.7 5.4 %gather_fusion = bf16[256,2048]{1,0:T(8,128)(2,1)} fusion(bf16[640,2048]{1,0:T(8,128)(2,1)} %reshape.234, s32[1024]{0:T(1024)S(1)} %pad_clamp_fusion), kind=kCustom, calls=%fused_computation | custom fusion | bytes 2098176 | tf_op jit(solution)/shard_map/jit(_take)/gather | solution.py:123
  251.2 2.7 %multiply_reduce_fusion = f32[32,2048]{1,0:T(8,128)S(1)} fusion(bf16[256,2048]{1,0:T(8,128)(2,1)} %gather_fusion, f32[32,8]{1,0:T(8,128)S(1)} %copy.28, pred[32,8]{1,0:T(8,128)(4,1)S(1)} %compare_and_fusion), kind=kLoop, calls=%fused_computation.25 | loop fusion | flops 2031616 | bytes 1312000 | tf_op jit(solution)/shard_map/reduce_sum | solution.py:125
  (62 shorter events, 8.8 us)
Async XLA Ops:
  6.5 156.2 %copy-start = (bf16[1,768,2048]{2,1,0:T(8,128)(2,1)S(1)}, bf16[1,768,2048]{2,1,0:T(8,128)(2,1)}, u32[]{:S(2)}) copy-start(bf16[1,768,2048]{2,1,0:T(8,128)(2,1)} %param.23) | copy-start | bytes 9437188
  12.0 4.8 %copy-start.7 = (f32[32,128]{1,0:T(8,128)S(1)}, f32[32,128]{1,0:T(8,128)}, u32[]{:S(2)}) copy-start(f32[32,128]{1,0:T(8,128)} %get-tuple-element.9) | copy-start | bytes 49156
  19.1 3.1 %copy-start.6 = (f32[32,128]{1,0:T(8,128)S(1)}, f32[32,128]{1,0:T(8,128)}, u32[]{:S(2)}) copy-start(f32[32,128]{1,0:T(8,128)} %get-tuple-element.12) | copy-start | bytes 49156
  19.1 3.5 %copy-start.2 = (f32[256,4096]{1,0:T(8,128)S(1)}, f32[256,4096]{1,0:T(8,128)}, u32[]{:S(2)}) copy-start(f32[256,4096]{1,0:T(8,128)} %get-tuple-element.32) | copy-start | bytes 12582916
  26.9 4.8 %copy-start.5 = (f32[32,128]{1,0:T(8,128)S(1)}, f32[32,128]{1,0:T(8,128)}, u32[]{:S(2)}) copy-start(f32[32,128]{1,0:T(8,128)} %get-tuple-element.11) | copy-start | bytes 49156
  34.0 3.5 %copy-start.1 = (f32[256,4096]{1,0:T(8,128)S(1)}, f32[256,4096]{1,0:T(8,128)}, u32[]{:S(2)}) copy-start(f32[256,4096]{1,0:T(8,128)} %get-tuple-element.28) | copy-start | bytes 12582916
  40.3 38.5 %copy-start.3 = (bf16[1,32,2048]{2,1,0:T(8,128)(2,1)S(1)}, bf16[1,32,2048]{2,1,0:T(8,128)(2,1)}, u32[]{:S(2)}) copy-start(bf16[1,32,2048]{2,1,0:T(8,128)(2,1)} %param.18) | copy-start | bytes 393220
  42.0 11.1 %all-to-all-start = ((bf16[32,4,1024]{2,0,1:T(8,128)(2,1)}), bf16[32,4,1024]{2,0,1:T(8,128)(2,1)S(1)}, u32[]{:S(2)}, u32[]{:S(2)}) async-start(bf16[32,4,1024]{2,0,1:T(8,128)(2,1)} %pad_maximum_fusion), calls=%async_computation | async-start | bytes 524288 | tf_op jit(solution)/shard_map/all_to_all | solution.py:76
  46.3 32.5 %reduce-scatter.2.cloned.1.call-start = ((), (), s32[]{:S(2)}) async-start(), calls=%async_computation.4 | async-start | bytes 655360 | tf_op jit(solution)/shard_map/reduce_scatter | solution.py:77
  177.9 9.2 %copy-start.8 = (f32[1,32,8]{1,2,0:T(8,128)S(1)}, f32[1,32,8]{1,2,0:T(8,128)}, u32[]{:S(2)}) copy-start(f32[1,32,8]{1,2,0:T(8,128)} %param.25) | copy-start | bytes 3076
  177.9 62.3 %all-to-all-start.2 = ((bf16[128,5,2048]{2,1,0:T(8,128)(2,1)}), bf16[128,5,2048]{2,1,0:T(8,128)(2,1)}, u32[]{:S(2)}, u32[]{:S(2)}) async-start(bf16[128,5,2048]{2,1,0:T(8,128)(2,1)} %reshape.233), calls=%async_computation.3 | async-start | bytes 8388608 | tf_op jit(solution)/shard_map/all_to_all | solution.py:116
  245.7 8.1 %copy-start.4 = (bf16[32,2048]{1,0:T(8,128)(2,1)S(1)}, bf16[32,2048]{1,0:T(8,128)(2,1)}, u32[]{:S(2)}) copy-start(bf16[32,2048]{1,0:T(8,128)(2,1)} %reduce-scatter.2.cloned.1.call-done) | copy-start | bytes 393220
Sparse Core Ops, SparseCore 0:
  56.9 21.8 reduce-scatter.1
where the time goes:
time: 265 us; the launch traced here: 261 us
  waiting for transfers between devices  75.7 us (29%)
  blocking collectives  62.3 us (24%)
  matrix products  44.3 us (17%)
  local copies, waits for them, and re-layouts  34.2 us (13%)
  other arithmetic  17.6 us (7%)
  between operations  13.7 us (5%)
  starting transfers between devices  13.5 us (5%)
    all_to_all x1, blocking collectives, per_device(): lax.all_to_all(send_rows, ('role', 'row', 'col'), split_axis=0, concat_ax...  62.3 us
    all_to_all x1, waiting for transfers between devices, per_device(): lax.all_to_all(result_rows.reshape(block.shape), ('role', 'row', 'col'),...  52.8 us
    reduce_scatter x1, waiting for transfers between devices, per_device(): lax.psum_scatter(jnp.dot(head_parts, out_weight, preferred_element_type=j...  19.7 us
    dot_general x4, matrix products, attend_prompt(): jnp.einsum('qd,kd->qk', q_block, k_block, preferred_element_type=jnp.floa...  11.8 us
    dot_general x1, matrix products, per_device(): jnp.dot(act, down_matrix, preferred_element_type=jnp.float32)  9.64 us
    dot_general x4, matrix products, attend_prompt(): mixed_rows = jnp.dot(weights, v_block, preferred_element_type=jnp.float32)  9.63 us
    all_to_all x1, starting transfers between devices, per_device(): lax.all_to_all(result_rows.reshape(block.shape), ('role', 'row', 'col'),...  9.14 us
    reduce_sum x4, other arithmetic, attend_prompt(): denominator = jnp.sum(exp_scores, axis=1) + own_exp  7.5 us
  transfers between devices with their start and end apart: 3, of which 3 were waited for; matrix products, arithmetic and copies ran while one was open for 2% of the time, Pallas kernels for 0%

commit v1 on v0

v1 whole, which is shorter than its diff:
```python
import functools

import jax
import jax.numpy as jnp
import numpy as np
from jax import lax
from jax.experimental import pallas as pl
from jax.experimental.pallas import tpu as pltpu
from jax.sharding import PartitionSpec as P

MESH = pl.DeviceIdType.MESH
BF, F32 = jnp.bfloat16, jnp.float32

D = 2048
HS = 128
GROUPS = 4
HPG = 8
ROWS = 32
T = 4096
FE = 768
CAP = 5
SLOTS = 16 * CAP
QR = ROWS * HPG
TC = 1024
NC = 4
FC = D // NC
YFIRST = (0,)
LOG2E = 1.4426950408889634


def where_am_i():
    r, x, col = lax.axis_index("role"), lax.axis_index("row"), lax.axis_index("col")
    return r, x, lax.div(col, 4), lax.rem(col, 4)


def up(v, j):
    return lax.rem(v + j, 4)


def remote(src, dst, send, recv, dev):
    return pltpu.make_async_remote_copy(
        src_ref=src, dst_ref=dst, send_sem=send, recv_sem=recv, device_id=dev, device_id_type=MESH
    )


def attention_body(q_ref, k_hbm, v_hbm, nk_ref, nv_ref, hid_ref, w_hbm, gain_ref, mid_ref, normed_ref,
                   kv, vv, wv, sc, a_out, a_in, p_out, p_in, ksem, vsem, wsem, as_sem, ar_sem, ps_sem, pr_sem):
    r, x, z, y = where_am_i()
    col = z * 4 + y
    loads = []
    for j in range(GROUPS):
        g = up(x, 1 + j)
        cols = pl.ds(pl.multiple_of(g * HS, HS), HS)
        ck = pltpu.make_async_copy(k_hbm.at[:, cols], kv.at[j], ksem.at[j])
        cv = pltpu.make_async_copy(v_hbm.at[:, cols], vv.at[j], vsem.at[j])
        ck.start()
        cv.start()
        loads.append((ck, cv))
        if j == 0:
            cw = pltpu.make_async_copy(w_hbm, wv, wsem)
            cw.start()

    barrier = pltpu.get_barrier_semaphore()
    for j in range(1, 4):
        pl.semaphore_signal(barrier, inc=1, device_id=(r, up(x, j), col), device_id_type=MESH)
    pl.semaphore_wait(barrier, 3)

    scale = HS ** -0.5 * LOG2E
    outs, backs = [], []

    def serve(j):
        outs[j].wait_recv()
        if j == 0:
            cw.wait()
        p_out[j] = jnp.dot(a_in[j], wv[...], preferred_element_type=F32).astype(BF)
        back = remote(p_out.at[j], p_in.at[j], ps_sem.at[j], pr_sem.at[j], (r, up(x, 3 - j), col))
        back.start()
        backs.append(back)

    for j in range(GROUPS):
        g = up(x, 1 + j)
        q = jnp.concatenate(
            [q_ref[:, pl.ds(pl.multiple_of(g * (HPG * HS) + h * HS, HS), HS)] for h in range(HPG)], axis=0
        )
        gcols = pl.ds(pl.multiple_of(g * HS, HS), HS)
        own_k = jnp.concatenate([nk_ref[:, gcols]] * HPG, axis=0)
        own_v = jnp.concatenate([nv_ref[:, gcols]] * HPG, axis=0)
        own = jnp.sum(q.astype(F32) * own_k.astype(F32), axis=1, keepdims=True)
        loads[j][0].wait()

        def qk(i, m):
            at = pl.ds(pl.multiple_of(i * TC, TC), TC)
            s = lax.dot_general(q, kv[j, at, :], (((1,), (1,)), ((), ())), preferred_element_type=F32)
            sc[:, at] = s
            for b in range(TC // HS):
                m = jnp.maximum(m, s[:, b * HS:(b + 1) * HS])
            return m

        m = lax.fori_loop(0, T // TC, qk, jnp.full((QR, HS), -jnp.inf, F32))
        top = jnp.maximum(jnp.max(m, axis=1, keepdims=True), own)
        if j >= 1:
            serve(j - 1)
        loads[j][1].wait()

        def pv(i, carry):
            acc, den = carry
            at = pl.ds(pl.multiple_of(i * TC, TC), TC)
            e = jnp.exp2((sc[:, at] - top) * scale)
            for b in range(TC // HS):
                den = den + e[:, b * HS:(b + 1) * HS]
            acc = acc + jnp.dot(e.astype(BF), vv[j, at, :], preferred_element_type=F32)
            return acc, den

        zero = jnp.zeros((QR, HS), F32)
        acc, den = lax.fori_loop(0, T // TC, pv, (zero, zero))
        own_e = jnp.exp2((own - top) * scale)
        total = jnp.sum(den, axis=1, keepdims=True) + own_e
        att = ((acc + own_e * own_v.astype(F32)) / total).astype(BF)
        for h in range(HPG):
            a_out[j, :, h * HS:(h + 1) * HS] = att[h * ROWS:(h + 1) * ROWS]
        if j < 3:
            cp = remote(a_out.at[j], a_in.at[j], as_sem.at[j], ar_sem.at[j], (r, g, col))
            cp.start()
            outs.append(cp)

    mid = hid_ref[...].astype(F32) + jnp.dot(a_out[3], wv[...], preferred_element_type=F32)
    for j in range(3):
        backs[j].wait_recv()
        mid = mid + p_in[j].astype(F32)
    mid_ref[...] = mid
    ms = jnp.mean(mid * mid, axis=1, keepdims=True)
    normed_ref[...] = (mid * lax.rsqrt(ms + 1e-6) * gain_ref[...]).astype(BF)
    for j in range(3):
        outs[j].wait_send()
        backs[j].wait_send()


ATT_SCRATCH = [
    pltpu.VMEM((GROUPS, T, HS), BF),
    pltpu.VMEM((GROUPS, T, HS), BF),
    pltpu.VMEM((HPG * HS, D), BF),
    pltpu.VMEM((QR, T), F32),
    pltpu.VMEM((GROUPS, ROWS, HPG * HS), BF),
    pltpu.VMEM((3, ROWS, HPG * HS), BF),
    pltpu.VMEM((3, ROWS, D), BF),
    pltpu.VMEM((3, ROWS, D), BF),
    pltpu.SemaphoreType.DMA((GROUPS,)),
    pltpu.SemaphoreType.DMA((GROUPS,)),
    pltpu.SemaphoreType.DMA,
    pltpu.SemaphoreType.DMA((3,)),
    pltpu.SemaphoreType.DMA((3,)),
    pltpu.SemaphoreType.DMA((3,)),
    pltpu.SemaphoreType.DMA((3,)),
]


def attention_call(q, k, v, nk, nv, hid, w, gain):
    vmem, hbm = pl.BlockSpec(memory_space=pltpu.VMEM), pl.BlockSpec(memory_space=pl.ANY)
    return pl.pallas_call(
        attention_body,
        out_shape=(jax.ShapeDtypeStruct((ROWS, D), F32), jax.ShapeDtypeStruct((ROWS, D), BF)),
        in_specs=[vmem, hbm, hbm, vmem, vmem, vmem, hbm, vmem],
        out_specs=(vmem, vmem),
        scratch_shapes=ATT_SCRATCH,
        compiler_params=pltpu.CompilerParams(
            collective_id=0, has_side_effects=True, vmem_limit_bytes=56 * 2**20
        ),
        name="attention",
    )(q, k, v, nk, nv, hid, w, gain)


def table_constants():
    j = np.arange(8 * SLOTS)
    d, p, s = j // SLOTS, (j % SLOTS) // CAP, j % CAP
    rows = np.zeros((8, 8 * SLOTS), np.int32)
    rows[0], rows[1], rows[2], rows[3] = d // 4, d % 4, p, s
    i = np.arange(SLOTS)
    want = np.where((i // CAP)[:, None] == (np.arange(512) // ROWS)[None, :], (i % CAP)[:, None], -7)
    return rows, want.astype(np.float32)


def expert_body(normed_ref, mid_ref, ids_ref, gates_ref, rows_ref, want_ref, wg_hbm, wu_hbm, wd_hbm, out_ref,
                gath, tab, pack, block, wg, wu, wd, gacc, uacc, act, res, ret, part, part_in, half, half_in,
                sel, comb, wsem, ts, tr, s1s, s1r, s2s, s2r, ls, lr, locs, bs, br, h1s, h1r, h2s, h2r):
    r, x, z, y = where_am_i()
    a = jnp.where(r == 0, z, x)
    l = jnp.where(r == 0, x, z)

    def at(role, l_, a_, y_):
        xx = jnp.where(r == 0, l_, a_)
        zz = jnp.where(r == 0, a_, l_)
        return (role, xx, zz * 4 + y_)

    wcopies = [
        pltpu.make_async_copy(wg_hbm, wg, wsem.at[0]),
        pltpu.make_async_copy(wu_hbm, wu, wsem.at[1]),
        pltpu.make_async_copy(wd_hbm, wd, wsem.at[2]),
    ]
    for cp in wcopies:
        cp.start()

    barrier = pltpu.get_barrier_semaphore()
    partners = []
    for j in range(1, 4):
        partners += [at(r, up(l, j), a, y), at(r, l, up(a, j), y), at(r, l, a, up(y, j)),
                     at(1 - r, up(l, j), a, y), at(1 - r, l, up(a, j), y)]
    partners.append(at(1 - r, l, a, y))
    for dev in partners:
        pl.semaphore_signal(barrier, inc=1, device_id=dev, device_id_type=MESH)
    pl.semaphore_wait(barrier, len(partners))

    lane = lax.broadcasted_iota(jnp.int32, (ROWS, 128), 1)
    named = jnp.zeros((ROWS, 128), F32)
    gate = jnp.zeros((ROWS, 128), F32)
    for k in range(8):
        hit = ids_ref[:, k:k + 1] == lane
        named = jnp.where(hit, 1.0, named)
        gate = jnp.where(hit, gates_ref[:, k:k + 1], gate)
    before = lax.broadcasted_iota(jnp.int32, (ROWS, ROWS), 0) > lax.broadcasted_iota(jnp.int32, (ROWS, ROWS), 1)
    rank = jnp.dot(jnp.where(before, 1.0, 0.0).astype(BF), named.astype(BF), preferred_element_type=F32)
    tab[y, a, :, 0:128] = jnp.where(named > 0, rank, -1.0).astype(BF)
    tab[y, a, :, 128:256] = gate.astype(BF)

    pend = []

    def go(cp):
        cp.start()
        pend.append(cp)
        return cp

    t1 = [go(remote(tab.at[y, a], tab.at[y, a], ts.at[j - 1], tr.at[j - 1], at(r, l, up(a, j), y))) for j in range(1, 4)]

    first = []
    for c in range(NC):
        gath[c, y, a] = normed_ref[:, c * FC:(c + 1) * FC]
        cps = []
        for j in range(1, 4):
            dev = at(r, l, a, up(y, j)) if c in YFIRST else at(r, l, up(a, j), y)
            cps.append(go(remote(gath.at[c, y, a], gath.at[c, y, a], s1s.at[c, j - 1], s1r.at[c, j - 1], dev)))
        first.append(cps)

    for cp in t1:
        cp.wait_recv()
    t2 = [go(remote(tab.at[y], tab.at[y], ts.at[j + 2], tr.at[j + 2], at(r, l, a, up(y, j)))) for j in range(1, 4)]

    second = []
    for c in range(NC):
        for cp in first[c]:
            cp.wait_recv()
        cps = []
        for j in range(1, 4):
            if c in YFIRST:
                ref, dev = gath.at[c, :, a], at(r, l, up(a, j), y)
            else:
                ref, dev = gath.at[c, y], at(r, l, a, up(y, j))
            cps.append(go(remote(ref, ref, s2s.at[c, j - 1], s2r.at[c, j - 1], dev)))
        second.append(cps)

    for cp in t2:
        cp.wait_recv()
    step = jnp.where(r == 0, 16, 4)
    base = jnp.where(r == 0, z * 4 + y, x * 16 + y)
    ranks = tab[:, :, :, 0:128].reshape(512, 128)
    gates = tab[:, :, :, 128:256].reshape(512, 128)
    d8 = lax.broadcasted_iota(jnp.int32, (8, 128), 0)
    e8 = lax.broadcasted_iota(jnp.int32, (8, 128), 1)
    pick = jnp.where(e8 == (d8 >> 2) * 64 + (d8 & 3) * step + base, 1.0, 0.0).astype(BF)
    by_lane = lax.dot_general(pick, ranks, (((1,), (1,)), ((), ())), preferred_element_type=F32)
    for d in range(8):
        sel[d * SLOTS:(d + 1) * SLOTS, :] = jnp.where(want_ref[...] == by_lane[d:d + 1, :], 1.0, 0.0).astype(BF)
    e_of = rows_ref[0:1, :] * 64 + rows_ref[1:2, :] * step + base
    spread = jnp.where(lax.broadcasted_iota(jnp.int32, (128, 8 * SLOTS), 0) == e_of, 1.0, 0.0).astype(BF)
    rank_at = jnp.dot(ranks, spread, preferred_element_type=F32)
    gate_at = jnp.dot(gates, spread, preferred_element_type=F32)
    prompt = lax.broadcasted_iota(jnp.int32, (512, 8 * SLOTS), 0) >> 5
    mine = (prompt == rows_ref[2:3, :]) & (rank_at == rows_ref[3:4, :].astype(F32))
    comb[...] = jnp.where(mine, gate_at, 0.0).astype(BF)

    src = r * 4 + l
    third, local = [], []

    def send_slots(c):
        for cp in second[c]:
            cp.wait_recv()
        rows = gath[c].reshape(512, FC)
        pack[c] = jnp.dot(sel[...], rows, preferred_element_type=F32).astype(BF).reshape(8, SLOTS, FC)
        cps = []
        for j in range(7):
            if j < 3:
                d, dev = r * 4 + up(l, j + 1), at(r, up(l, j + 1), a, y)
            else:
                d, dev = (1 - r) * 4 + up(l, j - 3), at(1 - r, up(l, j - 3), a, y)
            cps.append(go(remote(pack.at[c, d], block.at[c, src], ls.at[c, j], lr.at[c, j], dev)))
        third.append(cps)
        own = pltpu.make_async_copy(pack.at[c, src], block.at[c, src], locs.at[0, c])
        own.start()
        local.append(own)

    def gate_up(c):
        for cp in third[c]:
            cp.wait_recv()
        local[c].wait()
        if c == 0:
            wcopies[0].wait()
            wcopies[1].wait()
        rows = block[c].reshape(8 * SLOTS, FC)
        at_f = slice(c * FC, (c + 1) * FC)
        gp = jnp.dot(rows, wg[at_f, :], preferred_element_type=F32)
        upp = jnp.dot(rows, wu[at_f, :], preferred_element_type=F32)
        if c == 0:
            gacc[...] = gp
            uacc[...] = upp
        elif c < NC - 1:
            gacc[...] += gp
            uacc[...] += upp
        else:
            gp = gp + gacc[...]
            act[...] = (gp * jax.nn.sigmoid(gp) * (upp + uacc[...])).astype(BF)

    for c in range(NC):
        send_slots(c)
        if c >= 1:
            gate_up(c - 1)
    gate_up(NC - 1)

    wcopies[2].wait()
    back, b_local, h1, h2 = [], [], [], []

    def down(c):
        o = jnp.dot(act[...], wd[:, c * FC:(c + 1) * FC], preferred_element_type=F32).astype(BF)
        res[c] = o.reshape(8, SLOTS, FC)
        cps = []
        for j in range(7):
            if j < 3:
                s, d, dev = r * 4 + up(l, j + 1), r * 4 + l, at(r, up(l, j + 1), a, y)
            else:
                s, d, dev = (1 - r) * 4 + up(a, j - 3), r * 4 + a, at(1 - r, l, up(a, j - 3), y)
            cps.append(go(remote(res.at[c, s], ret.at[c, d], bs.at[c, j], br.at[c, j], dev)))
        back.append(cps)
        own = pltpu.make_async_copy(res.at[c, src], ret.at[c, src], locs.at[1, c])
        own.start()
        b_local.append(own)

    def combine(c):
        for cp in back[c]:
            cp.wait_recv()
        b_local[c].wait()
        o = jnp.dot(comb[...], ret[c].reshape(8 * SLOTS, FC), preferred_element_type=F32).astype(BF)
        part[c] = o.reshape(4, 4, ROWS, FC)
        cps = []
        for j in range(1, 4):
            if c in YFIRST:
                ref, dev = part.at[c, :, up(a, j)], at(r, l, up(a, j), y)
            else:
                ref, dev = part.at[c, up(y, j)], at(r, l, a, up(y, j))
            cps.append(go(remote(ref, part_in.at[c, j - 1], h1s.at[c, j - 1], h1r.at[c, j - 1], dev)))
        h1.append(cps)

    def sum_one(c):
        for cp in h1[c]:
            cp.wait_recv()
        own = part[c, :, a] if c in YFIRST else part[c, y]
        o = own.astype(F32)
        for j in range(3):
            o = o + part_in[c, j].astype(F32)
        half[c] = o.astype(BF)
        cps = []
        for j in range(1, 4):
            if c in YFIRST:
                q, dev = up(y, j), at(r, l, a, up(y, j))
            else:
                q, dev = up(a, j), at(r, l, up(a, j), y)
            cps.append(go(remote(half.at[c, q], half_in.at[c, j - 1], h2s.at[c, j - 1], h2r.at[c, j - 1], dev)))
        h2.append(cps)

    def sum_two(c):
        for cp in h2[c]:
            cp.wait_recv()
        o = half[c, y if c in YFIRST else a].astype(F32)
        for j in range(3):
            o = o + half_in[c, j].astype(F32)
        at_f = slice(c * FC, (c + 1) * FC)
        out_ref[:, at_f] = (mid_ref[:, at_f] + o).astype(BF)

    for t in range(NC + 3):
        if t < NC:
            down(t)
        if 0 <= t - 1 < NC:
            combine(t - 1)
        if 0 <= t - 2 < NC:
            sum_one(t - 2)
        if 0 <= t - 3 < NC:
            sum_two(t - 3)
    for cp in pend:
        cp.wait_send()


EXP_SCRATCH = [
    pltpu.VMEM((NC, 4, 4, ROWS, FC), BF),
    pltpu.VMEM((4, 4, ROWS, 256), BF),
    pltpu.VMEM((NC, 8, SLOTS, FC), BF),
    pltpu.VMEM((NC, 8, SLOTS, FC), BF),
    pltpu.VMEM((D, FE), BF),
    pltpu.VMEM((D, FE), BF),
    pltpu.VMEM((FE, D), BF),
    pltpu.VMEM((8 * SLOTS, FE), F32),
    pltpu.VMEM((8 * SLOTS, FE), F32),
    pltpu.VMEM((8 * SLOTS, FE), BF),
    pltpu.VMEM((NC, 8, SLOTS, FC), BF),
    pltpu.VMEM((NC, 8, SLOTS, FC), BF),
    pltpu.VMEM((NC, 4, 4, ROWS, FC), BF),
    pltpu.VMEM((NC, 3, 4, ROWS, FC), BF),
    pltpu.VMEM((NC, 4, ROWS, FC), BF),
    pltpu.VMEM((NC, 3, ROWS, FC), BF),
    pltpu.VMEM((8 * SLOTS, 512), BF),
    pltpu.VMEM((512, 8 * SLOTS), BF),
    pltpu.SemaphoreType.DMA((3,)),
    pltpu.SemaphoreType.DMA((6,)),
    pltpu.SemaphoreType.DMA((6,)),
    pltpu.SemaphoreType.DMA((NC, 3)),
    pltpu.SemaphoreType.DMA((NC, 3)),
    pltpu.SemaphoreType.DMA((NC, 3)),
    pltpu.SemaphoreType.DMA((NC, 3)),
    pltpu.SemaphoreType.DMA((NC, 7)),
    pltpu.SemaphoreType.DMA((NC, 7)),
    pltpu.SemaphoreType.DMA((2, NC)),
    pltpu.SemaphoreType.DMA((NC, 7)),
    pltpu.SemaphoreType.DMA((NC, 7)),
    pltpu.SemaphoreType.DMA((NC, 3)),
    pltpu.SemaphoreType.DMA((NC, 3)),
    pltpu.SemaphoreType.DMA((NC, 3)),
    pltpu.SemaphoreType.DMA((NC, 3)),
]


def expert_call(normed, mid, ids, gates, wg, wu, wd):
    vmem, hbm = pl.BlockSpec(memory_space=pltpu.VMEM), pl.BlockSpec(memory_space=pl.ANY)
    rows, want = table_constants()
    return pl.pallas_call(
        expert_body,
        out_shape=jax.ShapeDtypeStruct((ROWS, D), BF),
        in_specs=[vmem] * 6 + [hbm] * 3,
        out_specs=vmem,
        scratch_shapes=EXP_SCRATCH,
        compiler_params=pltpu.CompilerParams(
            collective_id=1, has_side_effects=True, vmem_limit_bytes=56 * 2**20
        ),
        name="experts",
    )(normed, mid, ids, gates, jnp.asarray(rows), jnp.asarray(want), wg, wu, wd)


def per_device(queries, cache_keys, prompt_value_cache, new_keys, fresh_token_values, hidden, out_weight, norm_gain,
               expert_gate, expert_up, expert_down, expert_ids, routing_gates):
    mid, normed = attention_call(
        queries[0], cache_keys[0], prompt_value_cache[0], new_keys[0], fresh_token_values[0], hidden[0], out_weight,
        norm_gain[None, :],
    )
    out = expert_call(normed, mid, expert_ids[0], routing_gates[0], expert_gate[0], expert_up[0], expert_down[0])
    return out[None]


def solution(mesh):
    split = P(("role", "row", "col"), None, None)
    return jax.shard_map(
        per_device,
        mesh=mesh,
        in_specs=(split,) * 6 + (P("row", None), P()) + (split,) * 5,
        out_specs=split,
        check_vma=False,
    )
```

time: 265 us -> 113 us (0.43); the launches traced: 261 us -> 112 us
  Pallas kernels: 0 us -> 108 us
  waiting for transfers between devices: 75.7 us -> 0 us
  blocking collectives: 62.3 us -> 0 us
  matrix products: 44.3 us -> 0 us
  local copies, waits for them, and re-layouts: 34.2 us -> 4.3 us
  other arithmetic: 17.6 us -> 0 us
  between operations: 13.7 us -> 0.02 us
  starting transfers between devices: 13.5 us -> 0 us
    pallas_call x0 -> x2, Pallas kernels: none -> 108 us  [the longest x1 79 us: expert_call(): pl.pallas_call(expert_body, out_shape=jax.ShapeDtypeStruct((ROWS, D), BF)...]
    all_to_all x1 -> x0, blocking collectives: 62.3 us -> none  [per_device(): lax.all_to_all(send_rows, ('role', 'row', 'col'), split_axis=0, concat_ax...]
    all_to_all x2 -> x0, waiting for transfers between devices: 56 us -> none  [the longest x1 52.8 us: per_device(): lax.all_to_all(result_rows.reshape(block.shape), ('role', 'row', 'col'),...]
    dot_general x12 -> x0, matrix products: 44.3 us -> none  [the longest x4 11.8 us: attend_prompt(): jnp.einsum('qd,kd->qk', q_block, k_block, preferred_element_type=jnp.floa...]
    reshape x8 -> x0, local copies, waits for them, and re-layouts: 22.2 us -> none  [the longest x1 5.6 us: per_device(): returned.reshape(experts * capacity, width)]
    reduce_scatter x1 -> x0, waiting for transfers between devices: 19.7 us -> none  [per_device(): lax.psum_scatter(jnp.dot(head_parts, out_weight, preferred_element_type=j...]
    all_to_all x2 -> x0, starting transfers between devices: 13.5 us -> none  [the longest x1 9.14 us: per_device(): lax.all_to_all(result_rows.reshape(block.shape), ('role', 'row', 'col'),...]
    reduce_sum x9 -> x0, other arithmetic: 12.4 us -> none  [the longest x4 7.5 us: attend_prompt(): denominator = jnp.sum(exp_scores, axis=1) + own_exp]
  transfers between devices with their start and end apart: 3 -> 0, of which waited for: 3 -> 0; matrix products, arithmetic and copies ran while one was open for 2% -> 0% of each run, Pallas kernels for 0% -> 0%
where the time goes in v1:
time: 113 us; the launch traced here: 112 us
  Pallas kernels  108 us (96%)
  local copies, waits for them, and re-layouts  4.3 us (4%)
    pallas_call x1, Pallas kernels, expert_call(): pl.pallas_call(expert_body, out_shape=jax.ShapeDtypeStruct((ROWS, D), BF)...  79 us
    pallas_call x1, Pallas kernels, attention_call(): pl.pallas_call(attention_body, out_shape=(jax.ShapeDtypeStruct((ROWS, D),...  29 us
    unnamed x3, local copies, waits for them, and re-layouts  4.3 us

profile of v1, /device:TPU:0, one launch (start us, length us, event | category | flops | bytes accessed | tf_op | source)
XLA Modules:
  0.0 112.3 jit_solution(17028453170665235093)
XLA Ops:
  0.0 1.4 %copy.16 = s32[1,32,8]{2,1,0:T(8,128)} copy(s32[1,32,8]{1,2,0:T(8,128)} %param.26) | data formatting | bytes 2048 | tf_op args[11]
  1.4 1.4 %copy.17 = f32[1,32,8]{2,1,0:T(8,128)} copy(f32[1,32,8]{1,2,0:T(8,128)} %param.27) | data formatting | bytes 2048 | tf_op args[12]
  2.7 29.0 %attention.1 = (f32[32,2048]{1,0:T(8,128)}, bf16[32,2048]{1,0:T(8,128)(2,1)}) custom-call(bf16[32,4096]{1,0:T(8,128)(2,1)} %bitcast.19, bf16[4096,512]{1,0:T(8,128)(2,1)} %bitcast.13, bf16[4096,512]{1,0:T(8,128)(2,1)} %bitcast.14, bf16[32,512]{1,0:T(8,128)(2,1)} %bitcast.23, bf16[32,512]{1,0:T(8,128)(2,1)} %bitcast.24, bf16[32,2048]{1,0:T(8,128)(2,1)} %bitcast.20, ...), custom_call_target="tpu_custom_call" | custom-call | tf_op jit(solution)/shard_map/attention/pallas_call | solution.py:159
  31.7 79.0 %experts.1 = bf16[32,2048]{1,0:T(8,128)(2,1)} custom-call(bf16[32,2048]{1,0:T(8,128)(2,1)} %get-tuple-element.7.normed_ref, f32[32,2048]{1,0:T(8,128)} %get-tuple-element.8.mid_ref, s32[32,8]{1,0:T(8,128)} %bitcast.21, f32[32,8]{1,0:T(8,128)} %bitcast.22, s32[8,640]{1,0:T(8,128)} %constant.4.clone.rows_ref, f32[80,512]{1,0:T(8,128)} %constant.5.clone.want_ref, ...), custom_call_target="tpu_custom_call" | custom-call | tf_op jit(solution)/shard_map/experts/pallas_call | solution.py:439
  110.7 1.6 %copy.19 = bf16[1,32,2048]{2,1,0:T(8,128)(2,1)} copy(bf16[1,32,2048]{2,1,0:T(8,128)(2,1)} %bitcast.18) | data formatting | bytes 262144

commit v2 on v1

v2 whole, which is shorter than its diff:
```python
import jax
import jax.numpy as jnp
from jax import lax
from jax.experimental import pallas as pl
from jax.experimental.pallas import tpu as pltpu
from jax.sharding import PartitionSpec as P

MESH = pl.DeviceIdType.MESH
BF, F32 = jnp.bfloat16, jnp.float32

D = 2048
HS = 128
GROUPS = 4
HPG = 8
ROWS = 32
T = 4096
FE = 768
CAP = 5
SLOTS = 16 * CAP
QR = ROWS * HPG
TC = 1024
NC = 4
FC = D // NC
YFIRST = (0,)
THROTTLE = True
VMEM_LIMIT = 60 * 2**20
LOG2E = 1.4426950408889634


def where_am_i():
    r, x, col = lax.axis_index("role"), lax.axis_index("row"), lax.axis_index("col")
    return r, x, lax.div(col, 4), lax.rem(col, 4)


def up(v, j):
    return lax.rem(v + j, 4)


def remote(src, dst, send, recv, dev):
    return pltpu.make_async_remote_copy(
        src_ref=src, dst_ref=dst, send_sem=send, recv_sem=recv, device_id=dev, device_id_type=MESH
    )


def layer_body(q_hbm, k_hbm, v_hbm, nk_hbm, nv_hbm, hid_hbm, w_hbm, gain_ref, ids_ref, gates_ref, wg_hbm, wu_hbm,
               wd_hbm, out_ref,
               qv, nkv, nvv, hidv, kv, vv, wv, sc, a_out, a_in, p_out, p_in, mid_ref,
               gath, tab, pack, block, wg, wu, wd, gacc, uacc, act, res, ret, part, part_in, half, half_in, sel, comb,
               insem, ksem, vsem, wsem, as_sem, ar_sem, ps_sem, pr_sem,
               ts, tr, s1s, s1r, s2s, s2r, ls, lr, locs, bs, br, h1s, h1r, h2s, h2r):
    r, x, z, y = where_am_i()
    col = z * 4 + y
    a = jnp.where(r == 0, z, x)
    l = jnp.where(r == 0, x, z)

    def at(role, l_, a_, y_):
        xx = jnp.where(r == 0, l_, a_)
        zz = jnp.where(r == 0, a_, l_)
        return (role, xx, zz * 4 + y_)

    def load(src, dst, sem):
        return pltpu.make_async_copy(src, dst, sem)

    kloads, vloads = [], []
    for j in range(GROUPS):
        cols = pl.ds(pl.multiple_of(up(x, 1 + j) * HS, HS), HS)
        kloads.append(load(k_hbm.at[:, cols], kv.at[j], ksem.at[j]))
        vloads.append(load(v_hbm.at[:, cols], vv.at[j], vsem.at[j]))
    ins = [load(q_hbm, qv, insem.at[0]), load(nk_hbm, nkv, insem.at[1]), load(nv_hbm, nvv, insem.at[2]),
           load(hid_hbm, hidv, insem.at[3])]
    cw = load(w_hbm, wv, wsem.at[3])
    wcopies = [load(wg_hbm, wg, wsem.at[0]), load(wu_hbm, wu, wsem.at[1]), load(wd_hbm, wd, wsem.at[2])]
    for cp in ins:
        cp.start()
    kloads[0].start()
    vloads[0].start()

    barrier = pltpu.get_barrier_semaphore()
    partners = [at(1 - r, l, a, y)]
    for j in range(1, 4):
        partners += [at(r, up(l, j), a, y), at(r, l, up(a, j), y), at(r, l, a, up(y, j)),
                     at(1 - r, up(l, j), a, y), at(1 - r, l, up(a, j), y)]
    for dev in partners:
        pl.semaphore_signal(barrier, inc=1, device_id=dev, device_id_type=MESH)

    lane = lax.broadcasted_iota(jnp.int32, (ROWS, 128), 1)
    named = jnp.zeros((ROWS, 128), F32)
    gate = jnp.zeros((ROWS, 128), F32)
    for k in range(8):
        hit = ids_ref[:, k:k + 1] == lane
        named = jnp.where(hit, 1.0, named)
        gate = jnp.where(hit, gates_ref[:, k:k + 1], gate)
    before = lax.broadcasted_iota(jnp.int32, (ROWS, ROWS), 0) > lax.broadcasted_iota(jnp.int32, (ROWS, ROWS), 1)
    rank = jnp.dot(jnp.where(before, 1.0, 0.0).astype(BF), named.astype(BF), preferred_element_type=F32)
    tab[y, a, :, 0:128] = jnp.where(named > 0, rank, -1.0).astype(BF)
    tab[y, a, :, 128:256] = gate.astype(BF)

    pl.semaphore_wait(barrier, len(partners))

    pend = []

    def go(cp):
        cp.start()
        pend.append(cp)
        return cp

    t1 = [go(remote(tab.at[y, a], tab.at[y, a], ts.at[j - 1], tr.at[j - 1], at(r, l, up(a, j), y))) for j in range(1, 4)]
    t2 = []

    scale = HS ** -0.5 * LOG2E
    outs, backs = [], []

    def serve(j):
        outs[j].wait_recv()
        if j == 0:
            cw.wait()
        p_out[j] = jnp.dot(a_in[j], wv[...], preferred_element_type=F32).astype(BF)
        backs.append(go(remote(p_out.at[j], p_in.at[j], ps_sem.at[j], pr_sem.at[j], (r, up(x, 3 - j), col))))

    for j in range(GROUPS):
        g = up(x, 1 + j)
        if j == 0:
            for cp in ins[:3]:
                cp.wait()
        q = jnp.concatenate(
            [qv[:, pl.ds(pl.multiple_of(g * (HPG * HS) + h * HS, HS), HS)] for h in range(HPG)], axis=0
        )
        gcols = pl.ds(pl.multiple_of(g * HS, HS), HS)
        own_k = jnp.concatenate([nkv[:, gcols]] * HPG, axis=0)
        own_v = jnp.concatenate([nvv[:, gcols]] * HPG, axis=0)
        own = jnp.sum(q.astype(F32) * own_k.astype(F32), axis=1, keepdims=True)
        kloads[j].wait()
        if j + 1 < GROUPS:
            kloads[j + 1].start()
            vloads[j + 1].start()
            if j == 0:
                cw.start()
        else:
            for cp in wcopies:
                cp.start()

        def qk(i, m):
            rows = pl.ds(pl.multiple_of(i * TC, TC), TC)
            s = lax.dot_general(q, kv[j, rows, :], (((1,), (1,)), ((), ())), preferred_element_type=F32)
            sc[:, rows] = s
            for b in range(TC // HS):
                m = jnp.maximum(m, s[:, b * HS:(b + 1) * HS])
            return m

        m = lax.fori_loop(0, T // TC, qk, jnp.full((QR, HS), -jnp.inf, F32))
        top = jnp.maximum(jnp.max(m, axis=1, keepdims=True), own)
        vloads[j].wait()

        def pv(i, carry):
            acc, den = carry
            rows = pl.ds(pl.multiple_of(i * TC, TC), TC)
            e = jnp.exp2((sc[:, rows] - top) * scale)
            for b in range(TC // HS):
                den = den + e[:, b * HS:(b + 1) * HS]
            acc = acc + jnp.dot(e.astype(BF), vv[j, rows, :], preferred_element_type=F32)
            return acc, den

        zero = jnp.zeros((QR, HS), F32)
        acc, den = lax.fori_loop(0, T // TC, pv, (zero, zero))
        own_e = jnp.exp2((own - top) * scale)
        total = jnp.sum(den, axis=1, keepdims=True) + own_e
        att = ((acc + own_e * own_v.astype(F32)) / total).astype(BF)
        for h in range(HPG):
            a_out[j, :, h * HS:(h + 1) * HS] = att[h * ROWS:(h + 1) * ROWS]
        if j < 3:
            outs.append(go(remote(a_out.at[j], a_in.at[j], as_sem.at[j], ar_sem.at[j], (r, g, col))))
        if j == 0:
            for cp in t1:
                cp.wait_recv()
            for i in range(1, 4):
                t2.append(go(remote(tab.at[y], tab.at[y], ts.at[i + 2], tr.at[i + 2], at(r, l, a, up(y, i)))))
        if j >= 1:
            serve(j - 1)

    ins[3].wait()
    mid = hidv[...].astype(F32) + jnp.dot(a_out[3], wv[...], preferred_element_type=F32)
    mid_ref[...] = mid

    for cp in t2:
        cp.wait_recv()
    step = jnp.where(r == 0, 16, 4)
    base = jnp.where(r == 0, z * 4 + y, x * 16 + y)
    ranks = tab[:, :, :, 0:128].reshape(512, 128)
    gates = tab[:, :, :, 128:256].reshape(512, 128)
    d8 = lax.broadcasted_iota(jnp.int32, (8, 128), 0)
    e8 = lax.broadcasted_iota(jnp.int32, (8, 128), 1)
    pick = jnp.where(e8 == (d8 >> 2) * 64 + (d8 & 3) * step + base, 1.0, 0.0).astype(BF)
    by_lane = lax.dot_general(pick, ranks, (((1,), (1,)), ((), ())), preferred_element_type=F32)
    slot = lax.broadcasted_iota(jnp.int32, (SLOTS, 512), 0)
    its_prompt = (slot * 205) >> 10
    same = its_prompt == (lax.broadcasted_iota(jnp.int32, (SLOTS, 512), 1) >> 5)
    want = jnp.where(same, slot - its_prompt * CAP, -7).astype(F32)
    for d in range(8):
        sel[d * SLOTS:(d + 1) * SLOTS, :] = jnp.where(want == by_lane[d:d + 1, :], 1.0, 0.0).astype(BF)
    lane_j = lax.broadcasted_iota(jnp.int32, (1, 8 * SLOTS), 1)
    d_of = (lane_j * 205) >> 14
    rem = lane_j - d_of * SLOTS
    p_of = (rem * 205) >> 10
    s_of = (rem - p_of * CAP).astype(F32)
    e_of = (d_of >> 2) * 64 + (d_of & 3) * step + base
    spread = jnp.where(lax.broadcasted_iota(jnp.int32, (128, 8 * SLOTS), 0) == e_of, 1.0, 0.0).astype(BF)
    rank_at = jnp.dot(ranks, spread, preferred_element_type=F32)
    gate_at = jnp.dot(gates, spread, preferred_element_type=F32)
    prompt = lax.broadcasted_iota(jnp.int32, (512, 8 * SLOTS), 0) >> 5
    comb[...] = jnp.where((prompt == p_of) & (rank_at == s_of), gate_at, 0.0).astype(BF)

    for j in range(3):
        backs[j].wait_recv()
    mid = mid_ref[...]
    for j in range(3):
        mid = mid + p_in[j].astype(F32)
    mid_ref[...] = mid
    ms = jnp.mean(mid * mid, axis=1, keepdims=True)
    normed = (mid * lax.rsqrt(ms + 1e-6) * gain_ref[...]).astype(BF)

    first = []
    for c in range(NC):
        gath[c, y, a] = normed[:, c * FC:(c + 1) * FC]
        cps = []
        for j in range(1, 4):
            dev = at(r, l, a, up(y, j)) if c in YFIRST else at(r, l, up(a, j), y)
            cps.append(go(remote(gath.at[c, y, a], gath.at[c, y, a], s1s.at[c, j - 1], s1r.at[c, j - 1], dev)))
        first.append(cps)

    second = [None] * NC

    def spread_second(c):
        for cp in first[c]:
            cp.wait_recv()
        cps = []
        for j in range(1, 4):
            if c in YFIRST:
                ref, dev = gath.at[c, :, a], at(r, l, up(a, j), y)
            else:
                ref, dev = gath.at[c, y], at(r, l, a, up(y, j))
            cps.append(go(remote(ref, ref, s2s.at[c, j - 1], s2r.at[c, j - 1], dev)))
        second[c] = cps

    src = r * 4 + l
    third, local = [None] * NC, [None] * NC

    def send_slots(c):
        for cp in second[c]:
            cp.wait_recv()
        rows = gath[c].reshape(512, FC)
        pack[c] = jnp.dot(sel[...], rows, preferred_element_type=F32).astype(BF).reshape(8, SLOTS, FC)
        cps = []
        for j in range(7):
            if j < 3:
                d, dev = r * 4 + up(l, j + 1), at(r, up(l, j + 1), a, y)
            else:
                d, dev = (1 - r) * 4 + up(l, j - 3), at(1 - r, up(l, j - 3), a, y)
            cps.append(go(remote(pack.at[c, d], block.at[c, src], ls.at[c, j], lr.at[c, j], dev)))
        third[c] = cps
        own = pltpu.make_async_copy(pack.at[c, src], block.at[c, src], locs.at[0, c])
        own.start()
        local[c] = own

    def gate_up(c, begin, end):
        for cp in third[c]:
            cp.wait_recv()
        local[c].wait()
        if begin:
            wcopies[0].wait()
            wcopies[1].wait()
        rows = block[c].reshape(8 * SLOTS, FC)
        at_f = slice(c * FC, (c + 1) * FC)
        gp = jnp.dot(rows, wg[at_f, :], preferred_element_type=F32)
        upp = jnp.dot(rows, wu[at_f, :], preferred_element_type=F32)
        if begin:
            gacc[...] = gp
            uacc[...] = upp
        elif not end:
            gacc[...] += gp
            uacc[...] += upp
        else:
            gp = gp + gacc[...]
            act[...] = (gp * jax.nn.sigmoid(gp) * (upp + uacc[...])).astype(BF)

    spread_second(1)
    spread_second(0)
    if not THROTTLE:
        spread_second(2)
        spread_second(3)
    for c in range(NC):
        send_slots(c)
        if THROTTLE and c + 2 < NC:
            for cp in second[c + 1]:
                cp.wait_send()
                pend[:] = [p for p in pend if p is not cp]
            spread_second(c + 2)
        if c >= 1:
            gate_up(c - 1, c == 1, False)
    gate_up(NC - 1, False, True)

    wcopies[2].wait()
    back, b_local, h1, h2 = [None] * NC, [None] * NC, [None] * NC, [None] * NC

    def down(c):
        o = jnp.dot(act[...], wd[:, c * FC:(c + 1) * FC], preferred_element_type=F32).astype(BF)
        res[c] = o.reshape(8, SLOTS, FC)
        cps = []
        for j in range(7):
            if j < 3:
                s, d, dev = r * 4 + up(l, j + 1), r * 4 + l, at(r, up(l, j + 1), a, y)
            else:
                s, d, dev = (1 - r) * 4 + up(a, j - 3), r * 4 + a, at(1 - r, l, up(a, j - 3), y)
            cps.append(go(remote(res.at[c, s], ret.at[c, d], bs.at[c, j], br.at[c, j], dev)))
        back[c] = cps
        own = pltpu.make_async_copy(res.at[c, src], ret.at[c, src], locs.at[1, c])
        own.start()
        b_local[c] = own

    def combine(c):
        for cp in back[c]:
            cp.wait_recv()
        b_local[c].wait()
        o = jnp.dot(comb[...], ret[c].reshape(8 * SLOTS, FC), preferred_element_type=F32).astype(BF)
        part[c] = o.reshape(4, 4, ROWS, FC)
        cps = []
        for j in range(1, 4):
            if c in YFIRST:
                ref, dev = part.at[c, :, up(a, j)], at(r, l, up(a, j), y)
            else:
                ref, dev = part.at[c, up(y, j)], at(r, l, a, up(y, j))
            cps.append(go(remote(ref, part_in.at[c, j - 1], h1s.at[c, j - 1], h1r.at[c, j - 1], dev)))
        h1[c] = cps

    def sum_one(c):
        for cp in h1[c]:
            cp.wait_recv()
        own = part[c, :, a] if c in YFIRST else part[c, y]
        o = own.astype(F32)
        for j in range(3):
            o = o + part_in[c, j].astype(F32)
        half[c] = o.astype(BF)
        cps = []
        for j in range(1, 4):
            if c in YFIRST:
                q, dev = up(y, j), at(r, l, a, up(y, j))
            else:
                q, dev = up(a, j), at(r, l, up(a, j), y)
            cps.append(go(remote(half.at[c, q], half_in.at[c, j - 1], h2s.at[c, j - 1], h2r.at[c, j - 1], dev)))
        h2[c] = cps

    def sum_two(c):
        for cp in h2[c]:
            cp.wait_recv()
        o = half[c, y if c in YFIRST else a].astype(F32)
        for j in range(3):
            o = o + half_in[c, j].astype(F32)
        at_f = slice(c * FC, (c + 1) * FC)
        out_ref[:, at_f] = (mid_ref[:, at_f] + o).astype(BF)

    order = list(range(1, NC)) + [0]
    stages = (down, combine, sum_one, sum_two)
    for t in range(NC + 3):
        for n, stage in enumerate(stages):
            if 0 <= t - n < NC:
                stage(order[t - n])
    for cp in pend:
        cp.wait_send()


def scratch():
    vm, dma = pltpu.VMEM, pltpu.SemaphoreType.DMA
    return [
        vm((ROWS, 4096), BF), vm((ROWS, 512), BF), vm((ROWS, 512), BF), vm((ROWS, D), BF),
        vm((GROUPS, T, HS), BF), vm((GROUPS, T, HS), BF), vm((HPG * HS, D), BF), vm((QR, T), F32),
        vm((GROUPS, ROWS, HPG * HS), BF), vm((3, ROWS, HPG * HS), BF), vm((3, ROWS, D), BF), vm((3, ROWS, D), BF),
        vm((ROWS, D), F32),
        vm((NC, 4, 4, ROWS, FC), BF), vm((4, 4, ROWS, 256), BF),
        vm((NC, 8, SLOTS, FC), BF), vm((NC, 8, SLOTS, FC), BF),
        vm((D, FE), BF), vm((D, FE), BF), vm((FE, D), BF),
        vm((8 * SLOTS, FE), F32), vm((8 * SLOTS, FE), F32), vm((8 * SLOTS, FE), BF),
        vm((NC, 8, SLOTS, FC), BF), vm((NC, 8, SLOTS, FC), BF),
        vm((NC, 4, 4, ROWS, FC), BF), vm((NC, 3, 4, ROWS, FC), BF), vm((NC, 4, ROWS, FC), BF), vm((NC, 3, ROWS, FC), BF),
        vm((8 * SLOTS, 512), BF), vm((512, 8 * SLOTS), BF),
        dma((4,)), dma((GROUPS,)), dma((GROUPS,)), dma((4,)), dma((3,)), dma((3,)), dma((3,)), dma((3,)),
        dma((6,)), dma((6,)), dma((NC, 3)), dma((NC, 3)), dma((NC, 3)), dma((NC, 3)), dma((NC, 7)), dma((NC, 7)),
        dma((2, NC)), dma((NC, 7)), dma((NC, 7)), dma((NC, 3)), dma((NC, 3)), dma((NC, 3)), dma((NC, 3)),
    ]


def layer_call(cid, *args):
    vmem, hbm = pl.BlockSpec(memory_space=pltpu.VMEM), pl.BlockSpec(memory_space=pl.ANY)
    return pl.pallas_call(
        layer_body,
        out_shape=jax.ShapeDtypeStruct((ROWS, D), BF),
        in_specs=[hbm] * 7 + [vmem] * 3 + [hbm] * 3,
        out_specs=vmem,
        scratch_shapes=scratch(),
        compiler_params=pltpu.CompilerParams(
            collective_id=cid, has_side_effects=True, vmem_limit_bytes=VMEM_LIMIT
        ),
        name="layer_%d" % cid,
    )(*args)


def per_device(queries, cache_keys, prompt_value_cache, new_keys, fresh_token_values, hidden, out_weight, norm_gain,
               expert_gate, expert_up, expert_down, expert_ids, routing_gates):
    out = layer_call(
        0, queries[0], cache_keys[0], prompt_value_cache[0], new_keys[0], fresh_token_values[0], hidden[0], out_weight,
        norm_gain[None, :], expert_ids[0], routing_gates[0], expert_gate[0], expert_up[0], expert_down[0],
    )
    return out[None]


def solution(mesh):
    split = P(("role", "row", "col"), None, None)
    return jax.shard_map(
        per_device,
        mesh=mesh,
        in_specs=(split,) * 6 + (P("row", None), P()) + (split,) * 5,
        out_specs=split,
        check_vma=False,
    )
```

time: 113 us -> 108 us (0.956)
  Pallas kernels: 108 us -> 103 us
    pallas_call x2 -> x1, Pallas kernels: 108 us -> 103 us  [layer_call(): pl.pallas_call(layer_body, out_shape=jax.ShapeDtypeStruct((ROWS, D), BF),...]
where the time goes in v2:
time: 108 us; the launch traced here: 107 us
  Pallas kernels  103 us (95%)
  local copies, waits for them, and re-layouts  4.29 us (4%)
    pallas_call x1, Pallas kernels, layer_call(): pl.pallas_call(layer_body, out_shape=jax.ShapeDtypeStruct((ROWS, D), BF),...  103 us
    unnamed x3, local copies, waits for them, and re-layouts  4.29 us

profile of v2, /device:TPU:0, one launch (start us, length us, event | category | flops | bytes accessed | tf_op | source)
XLA Modules:
  0.0 107.3 jit_solution(11642259167369785361)
XLA Ops:
  0.0 1.4 %copy.14 = s32[1,32,8]{2,1,0:T(8,128)} copy(s32[1,32,8]{1,2,0:T(8,128)} %param.24) | data formatting | bytes 2048 | tf_op args[11]
  1.4 1.4 %copy.15 = f32[1,32,8]{2,1,0:T(8,128)} copy(f32[1,32,8]{1,2,0:T(8,128)} %param.25) | data formatting | bytes 2048 | tf_op args[12]
  2.7 103.0 %layer_0.1 = bf16[32,2048]{1,0:T(8,128)(2,1)} custom-call(bf16[32,4096]{1,0:T(8,128)(2,1)} %bitcast.19, bf16[4096,512]{1,0:T(8,128)(2,1)} %bitcast.13, bf16[4096,512]{1,0:T(8,128)(2,1)} %bitcast.14, bf16[32,512]{1,0:T(8,128)(2,1)} %bitcast.23, bf16[32,512]{1,0:T(8,128)(2,1)} %bitcast.24, bf16[32,2048]{1,0:T(8,128)(2,1)} %bitcast.20, ...), custom_call_target="tpu_custom_call" | custom-call | tf_op jit(solution)/shard_map/layer_0/pallas_call | solution.py:392
  105.7 1.6 %copy.17 = bf16[1,32,2048]{2,1,0:T(8,128)(2,1)} copy(bf16[1,32,2048]{2,1,0:T(8,128)(2,1)} %bitcast.18) | data formatting | bytes 262144

commit v3 on v2

v3 whole, which is shorter than its diff:
```python
import jax
import jax.numpy as jnp
from jax import lax
from jax.experimental import pallas as pl
from jax.experimental.pallas import tpu as pltpu
from jax.sharding import PartitionSpec as P

MESH = pl.DeviceIdType.MESH
BF, F32 = jnp.bfloat16, jnp.float32

D = 2048
HS = 128
GROUPS = 4
HPG = 8
ROWS = 32
T = 4096
FE = 768
CAP = 5
SLOTS = 16 * CAP
QR = ROWS * HPG
TC = 1024
CHUNKS = ((0, 512, True), (512, 256, True), (768, 512, False), (1280, 512, False), (1792, 256, False))
TO_ORDER = (2, 0, 1, 3, 4)
SLOT_ORDER = (0, 1, 2, 3, 4)
BACK_ORDER = (4, 2, 3, 0, 1)
VMEM_LIMIT = 60 * 2**20
LOG2E = 1.4426950408889634


def where_am_i():
    r, x, col = lax.axis_index("role"), lax.axis_index("row"), lax.axis_index("col")
    return r, x, lax.div(col, 4), lax.rem(col, 4)


def up(v, j):
    return lax.rem(v + j, 4)


def remote(src, dst, send, recv, dev):
    return pltpu.make_async_remote_copy(
        src_ref=src, dst_ref=dst, send_sem=send, recv_sem=recv, device_id=dev, device_id_type=MESH
    )


def layer_body(q_hbm, k_hbm, v_hbm, nk_hbm, nv_hbm, hid_hbm, w_hbm, gain_ref, ids_ref, gates_ref, wg_hbm, wu_hbm,
               wd_hbm, out_ref,
               qv, nkv, nvv, hidv, kv, vv, wv, sc, a_out, a_in, p_out, p_in, mid_ref,
               tab, wg, wu, wd, gacc, uacc, act, sel, comb, gath, pack, block, res, ret, part, part_in, half, half_in,
               insem, ksem, vsem, wsem, as_sem, ar_sem, ps_sem, pr_sem,
               ts, tr, s1s, s1r, s2s, s2r, ls, lr, locs, bs, br, h1s, h1r, h2s, h2r):
    r, x, z, y = where_am_i()
    col = z * 4 + y
    a = jnp.where(r == 0, z, x)
    l = jnp.where(r == 0, x, z)

    def at(role, l_, a_, y_):
        xx = jnp.where(r == 0, l_, a_)
        zz = jnp.where(r == 0, a_, l_)
        return (role, xx, zz * 4 + y_)

    def load(src, dst, sem):
        return pltpu.make_async_copy(src, dst, sem)

    kloads, vloads = [], []
    for j in range(GROUPS):
        cols = pl.ds(pl.multiple_of(up(x, 1 + j) * HS, HS), HS)
        kloads.append(load(k_hbm.at[:, cols], kv.at[j], ksem.at[j]))
        vloads.append(load(v_hbm.at[:, cols], vv.at[j], vsem.at[j]))
    ins = [load(q_hbm, qv, insem.at[0]), load(nk_hbm, nkv, insem.at[1]), load(nv_hbm, nvv, insem.at[2]),
           load(hid_hbm, hidv, insem.at[3])]
    cw = load(w_hbm, wv, wsem.at[3])
    wcopies = [load(wg_hbm, wg, wsem.at[0]), load(wu_hbm, wu, wsem.at[1]), load(wd_hbm, wd, wsem.at[2])]
    for cp in ins:
        cp.start()
    kloads[0].start()
    vloads[0].start()
    kloads[1].start()

    barrier = pltpu.get_barrier_semaphore()
    partners = [at(1 - r, l, a, y)]
    for j in range(1, 4):
        partners += [at(r, up(l, j), a, y), at(r, l, up(a, j), y), at(r, l, a, up(y, j)),
                     at(1 - r, up(l, j), a, y), at(1 - r, l, up(a, j), y)]
    for dev in partners:
        pl.semaphore_signal(barrier, inc=1, device_id=dev, device_id_type=MESH)

    expert = lax.broadcasted_iota(jnp.int32, (128, ROWS), 0)
    named_t = jnp.zeros((128, ROWS), F32)
    gate_t = jnp.zeros((128, ROWS), F32)
    for k in range(8):
        hit = ids_ref[k:k + 1, :] == expert
        named_t = jnp.where(hit, 1.0, named_t)
        gate_t = jnp.where(hit, gates_ref[k:k + 1, :], gate_t)
    sq0 = lax.broadcasted_iota(jnp.int32, (ROWS, ROWS), 0)
    sq1 = lax.broadcasted_iota(jnp.int32, (ROWS, ROWS), 1)
    before = jnp.where(sq0 > sq1, 1.0, 0.0).astype(BF)
    same_row = jnp.where(sq0 == sq1, 1.0, 0.0).astype(BF)

    def rows_of(left, right):
        return lax.dot_general(left, right.astype(BF), (((1,), (1,)), ((), ())), preferred_element_type=F32)

    tab[y, a, :, 0:128] = jnp.where(rows_of(same_row, named_t) > 0, rows_of(before, named_t), -1.0).astype(BF)
    tab[y, a, :, 128:256] = rows_of(same_row, gate_t).astype(BF)

    pend = []

    def go(cp):
        cp.start()
        pend.append(cp)
        return cp

    t1, t2 = [], []

    scale = HS ** -0.5 * LOG2E
    outs, backs = [], []

    def serve(j):
        outs[j].wait_recv()
        if j == 0:
            cw.wait()
        p_out[j] = jnp.dot(a_in[j], wv[...], preferred_element_type=F32).astype(BF)
        backs.append(go(remote(p_out.at[j], p_in.at[j], ps_sem.at[j], pr_sem.at[j], (r, up(x, 3 - j), col))))

    def block_of(j):
        g = up(x, 1 + j)
        q = jnp.concatenate(
            [qv[:, pl.ds(pl.multiple_of(g * (HPG * HS) + h * HS, HS), HS)] for h in range(HPG)], axis=0
        )
        own_k = jnp.concatenate([nkv[:, pl.ds(pl.multiple_of(g * HS, HS), HS)]] * HPG, axis=0)
        return q, jnp.sum(q.astype(F32) * own_k.astype(F32), axis=1, keepdims=True)

    def keys_at(i):
        return pl.ds(pl.multiple_of(i * TC, TC), TC)

    def score(j, i, q, m):
        s = lax.dot_general(q, kv[j, keys_at(i), :], (((1,), (1,)), ((), ())), preferred_element_type=F32)
        sc[j % 2, :, keys_at(i)] = s
        for b in range(TC // HS):
            m = jnp.maximum(m, s[:, b * HS:(b + 1) * HS])
        return m

    def mix(j, i, top, acc, den):
        e = jnp.exp2((sc[j % 2, :, keys_at(i)] - top) * scale)
        for b in range(TC // HS):
            den = den + e[:, b * HS:(b + 1) * HS]
        return acc + jnp.dot(e.astype(BF), vv[j, keys_at(i), :], preferred_element_type=F32), den

    low, zero = jnp.full((QR, HS), -jnp.inf, F32), jnp.zeros((QR, HS), F32)
    for cp in ins[:3]:
        cp.wait()
    kloads[0].wait()
    q, own = block_of(0)
    m = lax.fori_loop(0, T // TC, lambda i, m: score(0, i, q, m), low)
    for j in range(GROUPS):
        g = up(x, 1 + j)
        own_v = jnp.concatenate([nvv[:, pl.ds(pl.multiple_of(g * HS, HS), HS)]] * HPG, axis=0)
        top = jnp.maximum(jnp.max(m, axis=1, keepdims=True), own)
        vloads[j].wait()
        if j + 2 < GROUPS:
            kloads[j + 2].start()
        if j + 1 < GROUPS:
            vloads[j + 1].start()
        if j == 0:
            cw.start()
        if j == 2:
            for cp in wcopies:
                cp.start()
        if j + 1 < GROUPS:
            kloads[j + 1].wait()
            q, next_own = block_of(j + 1)

            def both(i, carry):
                m, acc, den = carry
                m = score(j + 1, i, q, m)
                return m, *mix(j, i, top, acc, den)

            m, acc, den = lax.fori_loop(0, T // TC, both, (low, zero, zero))
        else:
            next_own = None
            acc, den = lax.fori_loop(0, T // TC, lambda i, carry: mix(j, i, top, *carry), (zero, zero))
        own_e = jnp.exp2((own - top) * scale)
        total = jnp.sum(den, axis=1, keepdims=True) + own_e
        att = ((acc + own_e * own_v.astype(F32)) / total).astype(BF)
        for h in range(HPG):
            a_out[j, :, h * HS:(h + 1) * HS] = att[h * ROWS:(h + 1) * ROWS]
        if j == 0:
            pl.semaphore_wait(barrier, len(partners))
        if j < 3:
            outs.append(go(remote(a_out.at[j], a_in.at[j], as_sem.at[j], ar_sem.at[j], (r, g, col))))
        if j == 0:
            for i in range(1, 4):
                t1.append(go(remote(tab.at[y, a], tab.at[y, a], ts.at[i - 1], tr.at[i - 1], at(r, l, up(a, i), y))))
        if j == 1:
            for cp in t1:
                cp.wait_recv()
            for i in range(1, 4):
                t2.append(go(remote(tab.at[y], tab.at[y], ts.at[i + 2], tr.at[i + 2], at(r, l, a, up(y, i)))))
        if j >= 1:
            serve(j - 1)
        own = next_own

    ins[3].wait()
    mid = hidv[...].astype(F32) + jnp.dot(a_out[3], wv[...], preferred_element_type=F32)
    mid_ref[...] = mid

    for cp in t2:
        cp.wait_recv()
    step = jnp.where(r == 0, 16, 4)
    base = jnp.where(r == 0, z * 4 + y, x * 16 + y)
    ranks = tab[:, :, :, 0:128].reshape(512, 128)
    gates = tab[:, :, :, 128:256].reshape(512, 128)
    d8 = lax.broadcasted_iota(jnp.int32, (8, 128), 0)
    e8 = lax.broadcasted_iota(jnp.int32, (8, 128), 1)
    pick = jnp.where(e8 == (d8 >> 2) * 64 + (d8 & 3) * step + base, 1.0, 0.0).astype(BF)
    by_lane = lax.dot_general(pick, ranks, (((1,), (1,)), ((), ())), preferred_element_type=F32)
    slot = lax.broadcasted_iota(jnp.int32, (SLOTS, 512), 0)
    its_prompt = (slot * 205) >> 10
    same = its_prompt == (lax.broadcasted_iota(jnp.int32, (SLOTS, 512), 1) >> 5)
    want = jnp.where(same, slot - its_prompt * CAP, -7).astype(F32)
    for d in range(8):
        sel[d * SLOTS:(d + 1) * SLOTS, :] = jnp.where(want == by_lane[d:d + 1, :], 1.0, 0.0).astype(BF)
    lane_j = lax.broadcasted_iota(jnp.int32, (1, 8 * SLOTS), 1)
    d_of = (lane_j * 205) >> 14
    rem = lane_j - d_of * SLOTS
    p_of = (rem * 205) >> 10
    s_of = (rem - p_of * CAP).astype(F32)
    e_of = (d_of >> 2) * 64 + (d_of & 3) * step + base
    spread = jnp.where(lax.broadcasted_iota(jnp.int32, (128, 8 * SLOTS), 0) == e_of, 1.0, 0.0).astype(BF)
    rank_at = jnp.dot(ranks, spread, preferred_element_type=F32)
    gate_at = jnp.dot(gates, spread, preferred_element_type=F32)
    prompt = lax.broadcasted_iota(jnp.int32, (512, 8 * SLOTS), 0) >> 5
    comb[...] = jnp.where((prompt == p_of) & (rank_at == s_of), gate_at, 0.0).astype(BF)

    for j in range(3):
        backs[j].wait_recv()
    mid = mid_ref[...]
    for j in range(3):
        mid = mid + p_in[j].astype(F32)
    mid_ref[...] = mid
    ms = jnp.mean(mid * mid, axis=1, keepdims=True)
    normed = (mid * lax.rsqrt(ms + 1e-6) * gain_ref[...]).astype(BF)

    def spots(c):
        def on_y(j):
            return up(y, j), at(r, l, a, up(y, j))

        def on_a(j):
            return up(a, j), at(r, l, up(a, j), y)

        return (a, y, on_a, on_y) if CHUNKS[c][2] else (y, a, on_y, on_a)

    first = [None] * len(CHUNKS)
    for c in TO_ORDER:
        m, n, _, inner = spots(c)
        gath[c][m, n] = normed[:, CHUNKS[c][0]:CHUNKS[c][0] + CHUNKS[c][1]]
        ref = gath[c].at[m, n]
        first[c] = [go(remote(ref, ref, s1s.at[c, j - 1], s1r.at[c, j - 1], inner(j)[1])) for j in range(1, 4)]

    second = [None] * len(CHUNKS)

    def spread_second(c):
        for cp in first[c]:
            cp.wait_recv()
        m, _, outer, _ = spots(c)
        ref = gath[c].at[m]
        second[c] = [go(remote(ref, ref, s2s.at[c, j - 1], s2r.at[c, j - 1], outer(j)[1])) for j in range(1, 4)]

    src = r * 4 + l
    third, local = [None] * len(CHUNKS), [None] * len(CHUNKS)

    def send_slots(c):
        fc = CHUNKS[c][1]
        for cp in second[c]:
            cp.wait_recv()
        if CHUNKS[c][2]:
            rows = jnp.concatenate([gath[c][i, k] for k in range(4) for i in range(4)], axis=0)
        else:
            rows = gath[c][...].reshape(512, fc)
        pack[c][...] = jnp.dot(sel[...], rows, preferred_element_type=F32).astype(BF).reshape(8, SLOTS, fc)
        cps = []
        for j in range(7):
            if j < 3:
                d, dev = r * 4 + up(l, j + 1), at(r, up(l, j + 1), a, y)
            else:
                d, dev = (1 - r) * 4 + up(l, j - 3), at(1 - r, up(l, j - 3), a, y)
            cps.append(go(remote(pack[c].at[d], block[c].at[src], ls.at[c, j], lr.at[c, j], dev)))
        third[c] = cps
        own = pltpu.make_async_copy(pack[c].at[src], block[c].at[src], locs.at[0, c])
        own.start()
        local[c] = own

    def gate_up(c, begin, end):
        fc = CHUNKS[c][1]
        for cp in third[c]:
            cp.wait_recv()
        local[c].wait()
        if begin:
            wcopies[0].wait()
            wcopies[1].wait()
        rows = block[c][...].reshape(8 * SLOTS, fc)
        at_f = slice(CHUNKS[c][0], CHUNKS[c][0] + CHUNKS[c][1])
        gp = jnp.dot(rows, wg[at_f, :], preferred_element_type=F32)
        upp = jnp.dot(rows, wu[at_f, :], preferred_element_type=F32)
        if begin:
            gacc[...] = gp
            uacc[...] = upp
        elif not end:
            gacc[...] += gp
            uacc[...] += upp
        else:
            gp = gp + gacc[...]
            act[...] = (gp * jax.nn.sigmoid(gp) * (upp + uacc[...])).astype(BF)

    for c in TO_ORDER:
        spread_second(c)
    last = len(CHUNKS) - 1
    for i, c in enumerate(SLOT_ORDER):
        send_slots(c)
        if i >= 1:
            gate_up(SLOT_ORDER[i - 1], i == 1, False)
    gate_up(SLOT_ORDER[last], False, True)

    wcopies[2].wait()
    back, b_local, h1, h2 = [None] * len(CHUNKS), [None] * len(CHUNKS), [None] * len(CHUNKS), [None] * len(CHUNKS)

    def down(c):
        f0, fc, _ = CHUNKS[c]
        o = jnp.dot(act[...], wd[:, f0:f0 + fc], preferred_element_type=F32).astype(BF)
        res[c][...] = o.reshape(8, SLOTS, fc)
        cps = []
        for j in range(7):
            if j < 3:
                s, d, dev = r * 4 + up(l, j + 1), r * 4 + l, at(r, up(l, j + 1), a, y)
            else:
                s, d, dev = (1 - r) * 4 + up(a, j - 3), r * 4 + a, at(1 - r, l, up(a, j - 3), y)
            cps.append(go(remote(res[c].at[s], ret[c].at[d], bs.at[c, j], br.at[c, j], dev)))
        back[c] = cps
        own = pltpu.make_async_copy(res[c].at[src], ret[c].at[src], locs.at[1, c])
        own.start()
        b_local[c] = own

    def combine(c):
        fc = CHUNKS[c][1]
        for cp in back[c]:
            cp.wait_recv()
        b_local[c].wait()
        o = jnp.dot(comb[...], ret[c][...].reshape(8 * SLOTS, fc), preferred_element_type=F32).astype(BF)
        if CHUNKS[c][2]:
            for p in range(16):
                part[c][p % 4, p // 4] = o[p * ROWS:(p + 1) * ROWS]
        else:
            part[c][...] = o.reshape(4, 4, ROWS, fc)
        _, _, outer, _ = spots(c)
        cps = []
        for j in range(1, 4):
            to, dev = outer(j)
            cps.append(go(remote(part[c].at[to], part_in[c].at[j - 1], h1s.at[c, j - 1], h1r.at[c, j - 1], dev)))
        h1[c] = cps

    def sum_one(c):
        for cp in h1[c]:
            cp.wait_recv()
        m, _, _, inner = spots(c)
        o = part[c][m].astype(F32)
        for j in range(3):
            o = o + part_in[c][j].astype(F32)
        half[c][...] = o.astype(BF)
        cps = []
        for j in range(1, 4):
            q, dev = inner(j)
            cps.append(go(remote(half[c].at[q], half_in[c].at[j - 1], h2s.at[c, j - 1], h2r.at[c, j - 1], dev)))
        h2[c] = cps

    def sum_two(c):
        for cp in h2[c]:
            cp.wait_recv()
        o = half[c][spots(c)[1]].astype(F32)
        for j in range(3):
            o = o + half_in[c][j].astype(F32)
        at_f = slice(CHUNKS[c][0], CHUNKS[c][0] + CHUNKS[c][1])
        out_ref[:, at_f] = (mid_ref[:, at_f] + o).astype(BF)

    stages = (down, combine, sum_one, sum_two)
    for t in range(len(CHUNKS) + 3):
        for n, stage in enumerate(stages):
            if 0 <= t - n < len(CHUNKS):
                stage(BACK_ORDER[t - n])
    for cp in pend:
        cp.wait_send()


def scratch():
    vm, dma, n = pltpu.VMEM, pltpu.SemaphoreType.DMA, len(CHUNKS)

    def each(*lead):
        return [vm((*lead, width), BF) for _, width, _ in CHUNKS]

    return [
        vm((ROWS, 4096), BF), vm((ROWS, 512), BF), vm((ROWS, 512), BF), vm((ROWS, D), BF),
        vm((GROUPS, T, HS), BF), vm((GROUPS, T, HS), BF), vm((HPG * HS, D), BF), vm((2, QR, T), F32),
        vm((GROUPS, ROWS, HPG * HS), BF), vm((3, ROWS, HPG * HS), BF), vm((3, ROWS, D), BF), vm((3, ROWS, D), BF),
        vm((ROWS, D), F32),
        vm((4, 4, ROWS, 256), BF), vm((D, FE), BF), vm((D, FE), BF), vm((FE, D), BF),
        vm((8 * SLOTS, FE), F32), vm((8 * SLOTS, FE), F32), vm((8 * SLOTS, FE), BF),
        vm((8 * SLOTS, 512), BF), vm((512, 8 * SLOTS), BF),
        each(4, 4, ROWS), each(8, SLOTS), each(8, SLOTS), each(8, SLOTS), each(8, SLOTS),
        each(4, 4, ROWS), each(3, 4, ROWS), each(4, ROWS), each(3, ROWS),
        dma((4,)), dma((GROUPS,)), dma((GROUPS,)), dma((4,)), dma((3,)), dma((3,)), dma((3,)), dma((3,)),
        dma((6,)), dma((6,)), dma((n, 3)), dma((n, 3)), dma((n, 3)), dma((n, 3)), dma((n, 7)), dma((n, 7)),
        dma((2, n)), dma((n, 7)), dma((n, 7)), dma((n, 3)), dma((n, 3)), dma((n, 3)), dma((n, 3)),
    ]


def layer_call(cid, *args):
    vmem, hbm = pl.BlockSpec(memory_space=pltpu.VMEM), pl.BlockSpec(memory_space=pl.ANY)
    return pl.pallas_call(
        layer_body,
        out_shape=jax.ShapeDtypeStruct((ROWS, D), BF),
        in_specs=[hbm] * 7 + [vmem] * 3 + [hbm] * 3,
        out_specs=vmem,
        scratch_shapes=scratch(),
        compiler_params=pltpu.CompilerParams(
            collective_id=cid, has_side_effects=True, vmem_limit_bytes=VMEM_LIMIT
        ),
        name="layer_%d" % cid,
    )(*args)


def per_device(queries, cache_keys, prompt_value_cache, new_keys, fresh_token_values, hidden, out_weight, norm_gain,
               expert_gate, expert_up, expert_down, expert_ids, routing_gates):
    out = layer_call(
        0, queries[0], cache_keys[0], prompt_value_cache[0], new_keys[0], fresh_token_values[0], hidden[0], out_weight,
        norm_gain[None, :], expert_ids[0].T, routing_gates[0].T, expert_gate[0], expert_up[0], expert_down[0],
    )
    return out[None]


def solution(mesh):
    split = P(("role", "row", "col"), None, None)
    return jax.shard_map(
        per_device,
        mesh=mesh,
        in_specs=(split,) * 6 + (P("row", None), P()) + (split,) * 5,
        out_specs=split,
        check_vma=False,
    )
```

time: 108 us -> 107 us (level)
  Pallas kernels: 103 us -> 106 us
  local copies, waits for them, and re-layouts: 4.29 us -> 1.57 us
    unnamed x3 -> x1, local copies, waits for them, and re-layouts: 4.29 us -> 1.57 us
    pallas_call x1, Pallas kernels: 103 us -> 106 us  [layer_call(): pl.pallas_call(layer_body, out_shape=jax.ShapeDtypeStruct((ROWS, D), BF),...]
where the time goes in v3:
time: 107 us
  Pallas kernels  106 us (99%)
  local copies, waits for them, and re-layouts  1.57 us (1%)
    pallas_call x1, Pallas kernels, layer_call(): pl.pallas_call(layer_body, out_shape=jax.ShapeDtypeStruct((ROWS, D), BF),...  106 us

profile of v3, /device:TPU:0, one launch (start us, length us, event | category | flops | bytes accessed | tf_op | source)
XLA Modules:
  0.0 107.2 jit_solution(3181115655123222849)
XLA Ops:
  0.0 105.7 %layer_0.1 = bf16[32,2048]{1,0:T(8,128)(2,1)} custom-call(bf16[32,4096]{1,0:T(8,128)(2,1)} %bitcast.23, bf16[4096,512]{1,0:T(8,128)(2,1)} %bitcast.17, bf16[4096,512]{1,0:T(8,128)(2,1)} %bitcast.18, bf16[32,512]{1,0:T(8,128)(2,1)} %bitcast.25, bf16[32,512]{1,0:T(8,128)(2,1)} %bitcast.26, bf16[32,2048]{1,0:T(8,128)(2,1)} %bitcast.24, ...), custom_call_target="tpu_custom_call" | custom-call | tf_op jit(solution)/shard_map/layer_0/pallas_call | solution.py:416
  105.7 1.6 %copy.15 = bf16[1,32,2048]{2,1,0:T(8,128)(2,1)} copy(bf16[1,32,2048]{2,1,0:T(8,128)(2,1)} %bitcast.22) | data formatting | bytes 262144

commit v4 on v3

--- a/solution.py
+++ b/solution.py
@@ -19,10 +19,10 @@
 SLOTS = 16 * CAP
 QR = ROWS * HPG
 TC = 1024
-CHUNKS = ((0, 512, True), (512, 256, True), (768, 512, False), (1280, 512, False), (1792, 256, False))
-TO_ORDER = (2, 0, 1, 3, 4)
-SLOT_ORDER = (0, 1, 2, 3, 4)
-BACK_ORDER = (4, 2, 3, 0, 1)
+CHUNKS = ((0, 768, True), (768, 768, False), (1536, 512, False))
+TO_ORDER = (1, 0, 2)
+SLOT_ORDER = (0, 1, 2)
+BACK_ORDER = (2, 1, 0)
 VMEM_LIMIT = 60 * 2**20
 LOG2E = 1.4426950408889634
 
@@ -33,7 +33,7 @@
 
 
 def up(v, j):
-    return lax.rem(v + j, 4)
+    return jnp.where(v + j > 3, v + j - 4, v + j)
 
 
 def remote(src, dst, send, recv, dev):
@@ -381,10 +381,17 @@
         out_ref[:, at_f] = (mid_ref[:, at_f] + o).astype(BF)
 
     stages = (down, combine, sum_one, sum_two)
+    sent = list(pend)
     for t in range(len(CHUNKS) + 3):
         for n, stage in enumerate(stages):
             if 0 <= t - n < len(CHUNKS):
                 stage(BACK_ORDER[t - n])
+                if t == 0 or (n == 2 and t - n == len(CHUNKS) - 1):
+                    sent = sent if t == 0 else pend[:-3]
+                    del pend[:len(sent)]
+                    for cp in sent:
+                        cp.wait_send()
+                    sent = []
     for cp in pend:
         cp.wait_send()
 

time: 107 us -> 102 us (0.953)
  Pallas kernels: 106 us -> 101 us
    pallas_call x1, Pallas kernels: 106 us -> 101 us  [layer_call(): pl.pallas_call(layer_body, out_shape=jax.ShapeDtypeStruct((ROWS, D), BF),...]
where the time goes in v4:
time: 102 us
  Pallas kernels  101 us (99%)
  local copies, waits for them, and re-layouts  1.57 us (2%)
    pallas_call x1, Pallas kernels, layer_call(): pl.pallas_call(layer_body, out_shape=jax.ShapeDtypeStruct((ROWS, D), BF),...  101 us

profile of v4, /device:TPU:0, one launch (start us, length us, event | category | flops | bytes accessed | tf_op | source)
XLA Modules:
  0.0 102.2 jit_solution(16016956096193245049)
XLA Ops:
  0.0 100.6 %layer_0.1 = bf16[32,2048]{1,0:T(8,128)(2,1)} custom-call(bf16[32,4096]{1,0:T(8,128)(2,1)} %bitcast.23, bf16[4096,512]{1,0:T(8,128)(2,1)} %bitcast.17, bf16[4096,512]{1,0:T(8,128)(2,1)} %bitcast.18, bf16[32,512]{1,0:T(8,128)(2,1)} %bitcast.25, bf16[32,512]{1,0:T(8,128)(2,1)} %bitcast.26, bf16[32,2048]{1,0:T(8,128)(2,1)} %bitcast.24, ...), custom_call_target="tpu_custom_call" | custom-call | tf_op jit(solution)/shard_map/layer_0/pallas_call | solution.py:423
  100.6 1.6 %copy.15 = bf16[1,32,2048]{2,1,0:T(8,128)(2,1)} copy(bf16[1,32,2048]{2,1,0:T(8,128)(2,1)} %bitcast.22) | data formatting | bytes 262144
